TPU v7x, 256 devices: a whole 4x4x8 slice. The times are simulated.
256 devices in a mesh: ty: 16 (over z_lo, x), tx: 16 (over z_hi, y, core).
Axes of the slice: x: 4, y: 4, z: 8 (z_hi: 2, z_lo: 4; z = z_hi * 4 + z_lo), core: 2. Of those that a mesh axis runs over, the one named last changes fastest.
Arguments:
- specimen: float32 [2, 8192, 8192], P(None, 'ty', 'tx'), may hold values from -3 to 3
- illumination: float32 [2, 256, 256], replicated, may hold values from -4 to 4
- patterns: float32 [16, 96, 256, 256], P('ty', 'tx'), may hold values from 0.05 to 2
- scan_offsets: int32 [16, 96, 2], P('ty', 'tx'), may hold values from 0 to 7936, as said below
- counts: int32 [16, 16], P('ty', 'tx'), may hold values from 1 to 6, as said below
Outputs:
- specimen_out: float32 [2, 8192, 8192], P(None, 'ty', 'tx')
- illumination_out: float32 [2, 256, 256], replicated
Inputs may be any that keep to these rules, and one draw needn't show every extreme that they name: `counts`: each tile has 1 to 6 live slots, and some tile has exactly 6. `scan_offsets`: the corner of every slot of tile (a, b) lies in that tile, and its 256 x 256 window lies inside the object.
All inputs are finite; a program needn't handle non-finite values.
Results may differ from a plain program's by a relative error of at most 0.0003.
Values sent between devices are 32-bit elements; how exact they have to be, the bound alone decides.
A program may use at most 128 MiB of HBM per device.

v0:
```python
import jax
import jax.numpy as jnp
from jax import lax
from jax.sharding import PartitionSpec as P

POS_DEV = 3
ITERS = 2


HIGHEST = lax.Precision.HIGHEST
OBJECT_STEP = 0.05
PROBE_GAIN = 0.5


def shifted(value, axis, steps):
    count = lax.axis_size(axis)
    initial, last = (max(0, -steps), min(count, count - steps))
    return lax.ppermute(value, axis, [(source, source + steps) for source in range(initial, last)])


def dft_tables(window):
    indices = jnp.arange(window, dtype=jnp.int32)
    products = indices[:, None] * indices[None, :] % window
    angles = products.astype(jnp.float32) * (2.0 * jnp.pi / window)
    scale = 1.0 / jnp.sqrt(jnp.float32(window))
    return (jnp.cos(angles) * scale, -jnp.sin(angles) * scale)


def complex_left(table_real, table_imag, batch_real, batch_imag):

    def apply_table(table, batch):
        return jnp.einsum("kn,snm->skm", table, batch, precision=HIGHEST)

    real_part = apply_table(table_real, batch_real) - apply_table(table_imag, batch_imag)
    imag_part = apply_table(table_real, batch_imag) + apply_table(table_imag, batch_real)
    return (real_part, imag_part)


def complex_right(batch_real, batch_imag, table_real, table_imag):

    def apply_table(batch, table):
        return jnp.einsum("skn,nm->skm", batch, table, precision=HIGHEST)

    real_part = apply_table(batch_real, table_real) - apply_table(batch_imag, table_imag)
    imag_part = apply_table(batch_imag, table_real) + apply_table(batch_real, table_imag)
    return (real_part, imag_part)


def extend_tile(specimen, window):
    rows_below = shifted(specimen[:, :window, :], "ty", -1)
    taller = jnp.concatenate([specimen, rows_below], axis=1)
    beside = shifted(taller[:, :, :window], "tx", -1)
    return jnp.concatenate([taller, beside], axis=2)


def fold_back(object_grad, window, tile_side):
    overflow = shifted(object_grad[:, :, tile_side:], "tx", 1)
    object_grad = object_grad.at[:, :, :window].add(overflow)
    overflow_down = shifted(object_grad[:, tile_side:, :tile_side], "ty", 1)
    return object_grad[:, :tile_side, :tile_side].at[:, :window, :].add(overflow_down)


def slot_gradients(
    extended, illumination, measured, row_offsets, column_offsets, active, dft_real, dft_imag
):
    window = illumination.shape[1]
    zero = jnp.zeros((), jnp.int32)

    def cut_window(corner_row, corner_col):
        return lax.dynamic_slice(extended, (zero, corner_row, corner_col), (2, window, window))

    patches = jax.vmap(cut_window)(row_offsets, column_offsets)
    patch_real = patches[:, 0]
    patch_imag = patches[:, 1]
    probe_real = illumination[0]
    probe_imag = illumination[1]
    psi_real = probe_real * patch_real - probe_imag * patch_imag
    psi_imag = probe_real * patch_imag + probe_imag * patch_real
    half_real, half_imag = complex_left(dft_real, dft_imag, psi_real, psi_imag)
    far_real, far_imag = complex_right(half_real, half_imag, dft_real, dft_imag)
    factor = active[:, None, None] * (far_real * far_real + far_imag * far_imag - measured)
    back_real, back_imag = complex_left(dft_real, -dft_imag, factor * far_real, factor * far_imag)
    chi_real, chi_imag = complex_right(back_real, back_imag, dft_real, -dft_imag)
    object_real = probe_real * chi_real + probe_imag * chi_imag
    object_imag = probe_real * chi_imag - probe_imag * chi_real
    probe_grad_real = jnp.sum(patch_real * chi_real + patch_imag * chi_imag, axis=0)
    probe_grad_imag = jnp.sum(patch_real * chi_imag - patch_imag * chi_real, axis=0)
    object_terms = jnp.stack([object_real, object_imag], axis=1)

    def add_slot(slot, accum):
        corner_row = row_offsets[slot]
        corner_col = column_offsets[slot]
        current = lax.dynamic_slice(accum, (zero, corner_row, corner_col), (2, window, window))
        return lax.dynamic_update_slice(
            accum, current + object_terms[slot], (zero, corner_row, corner_col)
        )

    object_grad = lax.fori_loop(
        0, object_terms.shape[0], add_slot, jnp.zeros(extended.shape, jnp.float32)
    )
    return (object_grad, jnp.stack([probe_grad_real, probe_grad_imag]))


def body(specimen, illumination, patterns, scan_offsets, counts):
    window = illumination.shape[1]
    tile_side = specimen.shape[1]
    slot_count = patterns.shape[1]
    row_anchor = lax.axis_index("ty") * tile_side
    column_anchor = lax.axis_index("tx") * tile_side
    row_offsets = scan_offsets[0, :, 0] - row_anchor
    column_offsets = scan_offsets[0, :, 1] - column_anchor
    active = (jnp.arange(slot_count, dtype=jnp.int32) < counts[0, 0]).astype(jnp.float32)
    measured = patterns[0]
    dft_real, dft_imag = dft_tables(window)
    device_count = lax.axis_size("ty") * lax.axis_size("tx")
    probe_step = PROBE_GAIN / (POS_DEV * device_count)
    for iteration in range(ITERS):
        extended = extend_tile(specimen, window)
        object_grad, probe_grad = slot_gradients(
            extended,
            illumination,
            measured,
            row_offsets,
            column_offsets,
            active,
            dft_real,
            dft_imag,
        )
        tile_grad = fold_back(object_grad, window, tile_side)
        probe_total = lax.psum(probe_grad, ("ty", "tx"))
        new_illumination = illumination - probe_step * probe_total
        specimen = specimen - OBJECT_STEP * tile_grad
        illumination = new_illumination
    return (specimen, illumination)


def solution(mesh):
    placed = (
        P(None, "ty", "tx"),
        P(),
        P("ty", "tx", None, None),
        P("ty", "tx", None),
        P("ty", "tx"),
    )
    return jax.shard_map(
        body, mesh=mesh, in_specs=placed, out_specs=(P(None, "ty", "tx"), P()), check_vma=False
    )
```

profile of v0, /device:TPU:198, one launch (start us, length us, event | category | flops | bytes accessed | tf_op | source)
XLA Modules:
  0.0 1073.2 jit_solution(6756833461963361991)
XLA Ops:
  11.6 26.0 %collective-permute-done = f32[2,256,512]{2,1,0:T(8,128)S(1)} collective-permute-done((f32[2,256,512]{2,1,0:T(8,128)S(1)}, f32[2,256,512]{2,1,0:T(8,128)S(1)}, u32[]{:S(2)}, u32[]{:S(2)}) %collective-permute-start) | collective-permute-done | bytes 1048608 | tf_op jit(solution)/shard_map/ppermute | solution.py:18
  39.0 3.5 collective-permute-start.1
  44.9 31.9 %collective-permute-done.1 = f32[2,768,256]{2,1,0:T(8,128)} collective-permute-done((f32[2,768,256]{2,1,0:T(8,128)}, f32[2,768,256]{2,1,0:T(8,128)}, u32[]{:S(2)}, u32[]{:S(2)}) %collective-permute-start.1) | collective-permute-done | bytes 1572896 | tf_op jit(solution)/shard_map/ppermute | solution.py:18
  76.9 3.9 pad_maximum_fusion
  81.1 19.7 %while.34 = (s32[]{:T(128)}, f32[2,768,768]{2,1,0:T(8,128)}, s32[6,3]{0,1:T(4,128)S(1)}, f32[6,2,256,256]{3,2,0,1:T(8,128)S(1)}, s32[]{:T(128)}) while((s32[]{:T(128)}, f32[2,768,768]{2,1,0:T(8,128)}, s32[6,3]{0,1:T(4,128)S(1)}, f32[6,2,256,256]{3,2,0,1:T(8,128)S(1)}, s32[]{:T(128)}) %tuple.115), condition=%wide.while_cond.4, body=%wide.while_body.4.sunk | while | flops 2 | bytes 1048693 | solution.py:70
  100.8 4.6 fusion.117
  105.4 3.7 fusion.114
  109.1 3.7 convolution_add_fusion.3
  112.8 3.8 fusion.32
  116.5 3.7 fusion.34
  120.2 3.7 convolution_subtract_fusion.3
  123.9 3.9 fusion.53
  127.9 4.2 fusion.49
  132.0 3.6 fusion.111
  135.7 4.0 fusion.108
  139.7 3.7 convolution_add_fusion.2
  143.4 3.6 fusion.22
  147.0 3.7 fusion.24
  150.7 3.8 convolution_subtract_fusion.2
  154.5 3.7 fusion.59
  158.2 5.4 fusion.43
  167.9 78.3 %while.32 = (s32[]{:T(128)}, f32[2,768,768]{2,1,0:T(8,128)}, s32[6]{0:T(128)S(1)}, s32[6]{0:T(128)S(1)}, f32[6,2,256,256]{3,2,0,1:T(8,128)}, /*index=5*/s32[]{:T(128)}, s32[]{:T(128)}, s32[]{:T(128)}) while((s32[]{:T(128)}, f32[2,768,768]{2,1,0:T(8,128)}, s32[6]{0:T(128)S(1)}, s32[6]{0:T(128)S(1)}, f32[6,2,256,256]{3,2,0,1:T(8,128)}, ...), condition=%wide.region_1.2_spmd, body=%wide.region_0.1_spmd.sunk | while | flops 131080 | bytes 2621633 | solution.py:98
  174.5 6.2 dynamic_update_slice.16
  187.3 6.5 dynamic_update_slice.16
  200.4 6.8 dynamic_update_slice.16
  213.8 6.5 dynamic_update_slice.16
  226.9 6.4 dynamic_update_slice.16
  239.9 6.3 dynamic_update_slice.16
  249.6 35.4 %collective-permute-done.2 = f32[2,768,256]{2,1,0:T(8,128)S(1)} collective-permute-done((f32[2,768,256]{2,1,0:T(8,128)S(1)}, f32[2,768,256]{2,1,0:T(8,128)S(1)}, u32[]{:S(2)}, u32[]{:S(2)}) %collective-permute-start.2) | collective-permute-done | bytes 1572896 | tf_op jit(solution)/shard_map/ppermute | solution.py:18
  292.8 13.0 %collective-permute-done.3 = f32[2,256,512]{2,1,0:T(8,128)S(1)} collective-permute-done((f32[2,256,512]{2,1,0:T(8,128)S(1)}, f32[2,256,512]{2,1,0:T(8,128)S(1)}, u32[]{:S(2)}, u32[]{:S(2)}) %collective-permute-start.3) | collective-permute-done | bytes 1048608 | tf_op jit(solution)/shard_map/ppermute | solution.py:18
  309.9 16.9 %collective-permute-done.4 = f32[2,256,512]{2,1,0:T(8,128)S(1)} collective-permute-done((f32[2,256,512]{2,1,0:T(8,128)S(1)}, f32[2,256,512]{2,1,0:T(8,128)S(1)}, u32[]{:S(2)}, u32[]{:S(2)}) %collective-permute-start.4) | collective-permute-done | bytes 1048608 | tf_op jit(solution)/shard_map/ppermute | solution.py:18
  331.3 245.9 %all-reduce.3.cloned.1.call-done = f32[2,256,256]{2,1,0:T(8,128)} async-done(((f32[2,256,256]{2,1,0:T(8,128)}), f32[2,256,256]{2,1,0:T(8,128)}) %all-reduce.3.cloned.1.call-update) | async-done | bytes 524304 | tf_op jit(solution)/shard_map/psum | solution.py:130
  578.3 4.2 pad_maximum_fusion.1
  584.5 24.7 %while.35 = (s32[]{:T(128)}, f32[2,768,768]{2,1,0:T(8,128)}, s32[6,3]{0,1:T(4,128)S(1)}, f32[6,2,256,256]{3,2,0,1:T(8,128)}, s32[]{:T(128)}) while((s32[]{:T(128)}, f32[2,768,768]{2,1,0:T(8,128)}, s32[6,3]{0,1:T(4,128)S(1)}, f32[6,2,256,256]{3,2,0,1:T(8,128)}, s32[]{:T(128)}) %tuple.131), condition=%wide.while_cond.5, body=%wide.while_body.5.sunk | while | flops 2 | bytes 1050217 | solution.py:70
  585.1 3.5 bitcast_dynamic-update-slice_fusion.5
  589.2 3.5 bitcast_dynamic-update-slice_fusion.5
  593.2 3.5 bitcast_dynamic-update-slice_fusion.5
  597.3 3.5 bitcast_dynamic-update-slice_fusion.5
  609.2 5.7 fusion.105
  614.9 3.7 fusion.102
  618.6 3.8 convolution_add_fusion.1
  622.4 3.8 fusion.8
  626.2 3.7 fusion.10
  629.8 3.7 convolution_subtract_fusion.1
  633.6 3.9 fusion.65
  637.5 4.2 fusion.47
  641.7 3.6 fusion.99
  645.3 4.1 fusion.96
  649.4 3.6 convolution_add_fusion
  653.0 3.6 fusion
  656.7 3.7 fusion.2
  660.4 3.8 convolution_subtract_fusion
  664.2 3.7 fusion.71
  667.8 5.2 fusion.19
  677.3 78.3 %while.33 = (s32[]{:T(128)}, f32[2,768,768]{2,1,0:T(8,128)}, s32[6]{0:T(128)S(1)}, s32[6]{0:T(128)S(1)}, f32[6,2,256,256]{3,2,0,1:T(8,128)}, /*index=5*/s32[]{:T(128)}, s32[]{:T(128)}, s32[]{:T(128)}) while((s32[]{:T(128)}, f32[2,768,768]{2,1,0:T(8,128)}, s32[6]{0:T(128)S(1)}, s32[6]{0:T(128)S(1)}, f32[6,2,256,256]{3,2,0,1:T(8,128)}, ...), condition=%wide.region_6.7_spmd, body=%wide.region_5.6_spmd.sunk | while | flops 131080 | bytes 2621633 | solution.py:98
  683.9 6.2 dynamic_update_slice.17
  696.7 6.5 dynamic_update_slice.17
  709.8 6.8 dynamic_update_slice.17
  723.2 6.5 dynamic_update_slice.17
  736.3 6.4 dynamic_update_slice.17
  749.3 6.3 dynamic_update_slice.17
  757.1 3.5 collective-permute-start.6
  760.6 44.8 %collective-permute-done.6 = f32[2,768,256]{2,1,0:T(8,128)S(1)} collective-permute-done((f32[2,768,256]{2,1,0:T(8,128)S(1)}, f32[2,768,256]{2,1,0:T(8,128)S(1)}, u32[]{:S(2)}, u32[]{:S(2)}) %collective-permute-start.6) | collective-permute-done | bytes 1572896 | tf_op jit(solution)/shard_map/ppermute | solution.py:18
  813.3 245.6 %all-reduce.5.cloned.1.call-done = f32[2,256,256]{2,1,0:T(8,128)} async-done(((f32[2,256,256]{2,1,0:T(8,128)}), f32[2,256,256]{2,1,0:T(8,128)}) %all-reduce.5.cloned.1.call-update) | async-done | bytes 524304 | tf_op jit(solution)/shard_map/psum | solution.py:130
  (139 shorter events, 118.5 us)
Async XLA Ops:
  7.2 570.0 %all-reduce.3.cloned.1.call-start = ((), (), s32[]{:S(2)}) async-start(), calls=%async_computation | async-start | bytes 1048576 | tf_op jit(solution)/shard_map/psum | solution.py:130
  7.2 4.2 copy-start.1
  8.7 28.9 %collective-permute-start = (f32[2,256,512]{2,1,0:T(8,128)S(1)}, f32[2,256,512]{2,1,0:T(8,128)S(1)}, u32[]{:S(2)}, u32[]{:S(2)}) collective-permute-start(f32[2,256,512]{2,1,0:T(8,128)S(1)} %slice.161), channel_id=1, source_target_pairs={{16,0},{32,16},{48,32},{64,48},{80,64},{96,80},{112,96},{128,112},... | collective-permute-start | bytes 3145736 | tf_op jit(solution)/shard_map/ppermute | solution.py:18
  37.6 5.5 copy-start.11
  39.0 37.9 %collective-permute-start.1 = (f32[2,768,256]{2,1,0:T(8,128)}, f32[2,768,256]{2,1,0:T(8,128)}, u32[]{:S(2)}, u32[]{:S(2)}) collective-permute-start(f32[2,768,256]{2,1,0:T(8,128)} %slice.212), channel_id=1, source_target_pairs={{1,0},{2,1},{3,2},{4,3},{5,4},{6,5},{7,6},{8,7},{9,8},{10,9},{11,1... | collective-permute-start | bytes 4718600 | tf_op jit(solution)/shard_map/ppermute | solution.py:18
  100.7 4.6 copy-start.3
  123.9 3.9 copy-start.4
  247.7 37.3 %collective-permute-start.2 = (f32[2,768,256]{2,1,0:T(8,128)S(1)}, f32[2,768,256]{2,1,0:T(8,128)S(1)}, u32[]{:S(2)}, u32[]{:S(2)}) collective-permute-start(f32[2,768,256]{2,1,0:T(8,128)S(1)} %slice.167), channel_id=1, source_target_pairs={{0,1},{1,2},{2,3},{3,4},{4,5},{5,6},{6,7},{7,8},{8,9},{9,10},{10,1... | collective-permute-start | bytes 4718600 | tf_op jit(solution)/shard_map/ppermute | solution.py:18
  289.1 16.7 %collective-permute-start.3 = (f32[2,256,512]{2,1,0:T(8,128)S(1)}, f32[2,256,512]{2,1,0:T(8,128)S(1)}, u32[]{:S(2)}, u32[]{:S(2)}) collective-permute-start(f32[2,256,512]{2,1,0:T(8,128)S(1)} %slice.215), channel_id=1, source_target_pairs={{0,16},{16,32},{32,48},{48,64},{64,80},{80,96},{96,112},{112,128},... | collective-permute-start | bytes 3145736 | tf_op jit(solution)/shard_map/ppermute | solution.py:18
  292.8 14.4 %copy-start.2 = (f32[2,512,512]{2,1,0:T(8,128)S(1)}, f32[2,512,512]{2,1,0:T(8,128)}, u32[]{:S(2)}) copy-start(f32[2,512,512]{2,1,0:T(8,128)} %param.17) | copy-start | bytes 6291460
  307.8 22.5 %copy-start.8 = (f32[256,256]{1,0:T(8,128)S(1)}, f32[256,256]{1,0:T(8,128)}, u32[]{:S(2)}) copy-start(f32[256,256]{1,0:T(8,128)} %get-tuple-element.268) | copy-start | bytes 786436
  307.8 22.5 %copy-start.9 = (f32[256,256]{1,0:T(8,128)S(1)}, f32[256,256]{1,0:T(8,128)}, u32[]{:S(2)}) copy-start(f32[256,256]{1,0:T(8,128)} %get-tuple-element.269) | copy-start | bytes 786436
  307.8 18.9 %collective-permute-start.4 = (f32[2,256,512]{2,1,0:T(8,128)S(1)}, f32[2,256,512]{2,1,0:T(8,128)S(1)}, u32[]{:S(2)}, u32[]{:S(2)}) collective-permute-start(f32[2,256,512]{2,1,0:T(8,128)S(1)} %slice.217), channel_id=1, source_target_pairs={{16,0},{32,16},{48,32},{64,48},{80,64},{96,80},{112,96},{128,112},... | collective-permute-start | bytes 3145736 | tf_op jit(solution)/shard_map/ppermute | solution.py:18
  326.8 1.5 copy-start.6
  328.3 248.8 %copy-start.7 = (f32[2,256,256]{2,1,0:T(8,128)S(1)}, f32[2,256,256]{2,1,0:T(8,128)}, u32[]{:S(2)}) copy-start(f32[2,256,256]{2,1,0:T(8,128)} %param.18) | copy-start | bytes 1572868
  328.3 250.0 %collective-permute-start.5 = (f32[2,768,256]{2,1,0:T(8,128)}, f32[2,768,256]{2,1,0:T(8,128)}, u32[]{:S(2)}, u32[]{:S(2)}) collective-permute-start(f32[2,768,256]{2,1,0:T(8,128)} %pad_maximum_fusion.4), channel_id=1, source_target_pairs={{1,0},{2,1},{3,2},{4,3},{5,4},{6,5},{7,6},{8,7},{9,8},{10,9},{11,1... | collective-permute-start | bytes 4718600 | tf_op jit(solution)/shard_map/ppermute | solution.py:18
  331.2 727.7 %all-reduce.5.cloned.1.call-start = ((), (), s32[]{:S(2)}) async-start(), calls=%async_computation.1 | async-start | bytes 1048576 | tf_op jit(solution)/shard_map/psum | solution.py:130
  609.2 5.7 copy-start
  633.6 3.9 copy-start.5
  757.1 48.3 %collective-permute-start.6 = (f32[2,768,256]{2,1,0:T(8,128)S(1)}, f32[2,768,256]{2,1,0:T(8,128)S(1)}, u32[]{:S(2)}, u32[]{:S(2)}) collective-permute-start(f32[2,768,256]{2,1,0:T(8,128)S(1)} %slice.178), channel_id=1, source_target_pairs={{0,1},{1,2},{2,3},{3,4},{4,5},{5,6},{6,7},{7,8},{8,9},{9,10},{10,1... | collective-permute-start | bytes 4718600 | tf_op jit(solution)/shard_map/ppermute | solution.py:18
  808.2 4.2 copy-start.10
  810.5 252.1 %collective-permute-start.7 = (f32[2,256,512]{2,1,0:T(8,128)}, f32[2,256,512]{2,1,0:T(8,128)}, u32[]{:S(2)}, u32[]{:S(2)}) collective-permute-start(f32[2,256,512]{2,1,0:T(8,128)} %slice.221), channel_id=1, source_target_pairs={{0,16},{16,32},{32,48},{48,64},{64,80},{80,96},{96,112},{112,128},... | collective-permute-start | bytes 3145736 | tf_op jit(solution)/shard_map/ppermute | solution.py:18
Sparse Core Ops, SparseCore 0:
  331.3 245.7 all-reduce.2
  813.4 245.4 all-reduce.4
where the time goes:
time: 1090 us; the launch traced here: 1070 us
  waiting for transfers between devices  659 us (60%)
  local copies, waits for them, and re-layouts  158 us (14%)
  matrix products  126 us (12%)
  other arithmetic  47.6 us (4%)
  loops' own time  47.2 us (4%)
  starting transfers between devices  19.6 us (2%)
  between operations  15.5 us (1%)
    psum x2, waiting for transfers between devices, body(): probe_total = lax.psum(probe_grad, ('ty', 'tx'))  491 us
    ppermute x8, waiting for transfers between devices, shifted(): lax.ppermute(value, axis, [(source, source + steps) for source in range(i...  168 us
    dynamic_update_slice x12, local copies, waits for them, and re-layouts, add_slot(): lax.dynamic_update_slice(accum, current + object_terms[slot], (zero, corn...  77.4 us
    dot_general x16, matrix products, apply_table(): return jnp.einsum('skn,nm->skm', batch, table, precision=HIGHEST)  63.5 us
    dot_general x16, matrix products, apply_table(): return jnp.einsum('kn,snm->skm', table, batch, precision=HIGHEST)  62.8 us
    another operation x2, loops' own time, slot_gradients(): lax.fori_loop(0, object_terms.shape[0], add_slot, jnp.zeros(extended.shap...  46.7 us
    gather x36, local copies, waits for them, and re-layouts  43.9 us
  transfers between devices with their start and end apart: 10, of which 8 were waited for; matrix products, arithmetic and copies ran while one was open for 1% of the time, Pallas kernels for 0%

commit v1 on v0

v1 whole, which is shorter than its diff:
```python
import functools

import jax
import jax.numpy as jnp
import ml_dtypes
import numpy as np
from jax import lax
from jax.experimental import pallas as pl
from jax.experimental.pallas import tpu as pltpu
from jax.sharding import PartitionSpec as P

POS_DEV = 3
ITERS = 2
OBJECT_STEP = 0.05
PROBE_GAIN = 0.5
MESH = pl.DeviceIdType.MESH
VMEM_LIMIT = 48 * 1024 * 1024
SUBLANES = 8


def real_table(window):
    half = window // 2
    k = np.arange(window)
    freq = np.where(k <= half, k, k - half)
    angles = 2.0 * np.pi * ((freq[:, None] * k[None, :]) % window) / window
    table = np.where((k <= half)[:, None], np.cos(angles), np.sin(angles))
    return table / np.sqrt(window)


def split_table(table):
    high = table.astype(ml_dtypes.bfloat16)
    low = (table - high.astype(np.float64)).astype(ml_dtypes.bfloat16)
    return high, low


def tables(window):
    high, low = split_table(real_table(window))
    left = np.concatenate([high, low, high], axis=1)
    left_back = np.concatenate([high.T, low.T, high.T], axis=1)
    right = np.concatenate([high.T, low.T, high.T], axis=0)
    right_back = np.concatenate([high, low, high], axis=0)
    return [jnp.asarray(t) for t in (left, right, left_back, right_back)]


def reorder_table(window):
    half = window // 2
    i = np.arange(window)
    freq = np.where(i <= half, i, window + half - i)
    return jnp.asarray((freq[:, None] == i[None, :]).astype(ml_dtypes.bfloat16))


def split(value):
    high = value.astype(jnp.bfloat16)
    low = (value - high.astype(jnp.float32)).astype(jnp.bfloat16)
    return high, low


def left_product(table, value):
    high, low = split(value)
    return jnp.dot(
        table, jnp.concatenate([high, high, low], axis=0), preferred_element_type=jnp.float32
    )


def right_product(value, table):
    high, low = split(value)
    return jnp.dot(
        jnp.concatenate([high, high, low], axis=1), table, preferred_element_type=jnp.float32
    )


def compute_kernel(
    count_ref, offsets_ref, specimen_ref, probe_ref, measured_ref,
    left_ref, right_ref, left_back_ref, right_back_ref,
    grad_ref, probe_grad_ref,
):
    window = probe_ref.shape[1]
    half = window // 2
    lanes = 128
    blocks = window // lanes
    grad_ref[...] = jnp.zeros_like(grad_ref)
    probe_grad_ref[...] = jnp.zeros_like(probe_grad_ref)
    lane = lax.broadcasted_iota(jnp.int32, (window + SUBLANES, lanes), 1)
    sublane = lax.broadcasted_iota(jnp.int32, (window // SUBLANES, SUBLANES, lanes), 1)
    sublane_ext = lax.broadcasted_iota(jnp.int32, (window // SUBLANES + 1, SUBLANES, lanes), 1)
    first_row = lax.broadcasted_iota(jnp.int32, (half, window), 0) == 0
    first_col = lax.broadcasted_iota(jnp.int32, (window, half), 1) == 0

    def visit(slot, carry):
        row = offsets_ref[slot, 0]
        col = offsets_ref[slot, 1]
        row_block = pl.multiple_of((row // SUBLANES) * SUBLANES, SUBLANES)
        col_block = pl.multiple_of((col // lanes) * lanes, lanes)
        row_rest = row - row_block
        col_rest = col - col_block

        def place(part, j):
            return (
                part,
                pl.ds(row_block, window + SUBLANES),
                pl.ds(pl.multiple_of(col_block + lanes * j, lanes), lanes),
            )

        def cut(part):
            keep = lane < lanes - col_rest
            pieces = [
                pltpu.roll(specimen_ref[place(part, j)], lax.rem(lanes - col_rest, lanes), 1)
                for j in range(blocks + 1)
            ]
            columns = []
            for j in range(blocks):
                taken = jnp.where(keep, pieces[j], pieces[j + 1])
                taken = taken.reshape(window // SUBLANES + 1, SUBLANES, lanes)
                taken = pltpu.roll(taken, lax.rem(SUBLANES - row_rest, SUBLANES), 1)
                upper = sublane < SUBLANES - row_rest
                columns.append(jnp.where(upper, taken[:-1], taken[1:]).reshape(window, lanes))
            return jnp.concatenate(columns, axis=1)

        patch_real, patch_imag = cut(0), cut(1)
        probe_real, probe_imag = probe_ref[0], probe_ref[1]
        psi_real = probe_real * patch_real - probe_imag * patch_imag
        psi_imag = probe_real * patch_imag + probe_imag * patch_real

        both = left_product(left_ref[...], jnp.concatenate([psi_real, psi_imag], axis=1))
        u_top, v_top = both[:half, :window], both[:half, window:]
        u_bot, v_bot = both[half:, :window], both[half:, window:]
        u_add = jnp.where(first_row, 0.0, u_bot)
        v_add = jnp.where(first_row, 0.0, v_bot)
        mid_real = jnp.concatenate([u_top + v_add, jnp.where(first_row, u_bot, u_top - v_bot)], axis=0)
        mid_imag = jnp.concatenate([v_top - u_add, jnp.where(first_row, v_bot, v_top + u_bot)], axis=0)

        both = right_product(jnp.concatenate([mid_real, mid_imag], axis=0), right_ref[...])
        u_top, v_top = both[:window, :half], both[window:, :half]
        u_bot, v_bot = both[:window, half:], both[window:, half:]
        u_add = jnp.where(first_col, 0.0, u_bot)
        v_add = jnp.where(first_col, 0.0, v_bot)
        far_real = jnp.concatenate([u_top + v_add, jnp.where(first_col, u_bot, u_top - v_bot)], axis=1)
        far_imag = jnp.concatenate([v_top - u_add, jnp.where(first_col, v_bot, v_top + u_bot)], axis=1)

        factor = far_real * far_real + far_imag * far_imag - measured_ref[slot]
        g_real = factor * far_real
        g_imag = factor * far_imag

        r_top, r_bot = g_real[:half], g_real[half:]
        i_top, i_bot = g_imag[:half], g_imag[half:]
        z_real = jnp.concatenate(
            [r_top + jnp.where(first_row, 0.0, r_bot), jnp.where(first_row, r_bot, i_bot - i_top)], axis=0)
        z_imag = jnp.concatenate(
            [i_top + jnp.where(first_row, 0.0, i_bot), jnp.where(first_row, i_bot, r_top - r_bot)], axis=0)
        both = left_product(left_back_ref[...], jnp.concatenate([z_real, z_imag], axis=1))

        r_top, r_bot = both[:, :half], both[:, half:window]
        i_top, i_bot = both[:, window:window + half], both[:, window + half:]
        z_real = jnp.concatenate(
            [r_top + jnp.where(first_col, 0.0, r_bot), jnp.where(first_col, r_bot, i_bot - i_top)], axis=1)
        z_imag = jnp.concatenate(
            [i_top + jnp.where(first_col, 0.0, i_bot), jnp.where(first_col, i_bot, r_top - r_bot)], axis=1)
        both = right_product(jnp.concatenate([z_real, z_imag], axis=0), right_back_ref[...])
        chi_real, chi_imag = both[:window], both[window:]

        probe_grad_ref[0] += patch_real * chi_real + patch_imag * chi_imag
        probe_grad_ref[1] += patch_real * chi_imag - patch_imag * chi_real
        terms = (
            probe_real * chi_real + probe_imag * chi_imag,
            probe_real * chi_imag - probe_imag * chi_real,
        )
        before = lane < col_rest
        above = sublane_ext < row_rest
        for part in range(2):
            turned = []
            for j in range(blocks):
                piece = terms[part][:, lanes * j:lanes * (j + 1)]
                piece = piece.reshape(window // SUBLANES, SUBLANES, lanes)
                piece = pltpu.roll(piece, row_rest, 1)
                edge = jnp.zeros((1, SUBLANES, lanes), jnp.float32)
                piece = jnp.where(
                    above,
                    jnp.concatenate([edge, piece], axis=0),
                    jnp.concatenate([piece, edge], axis=0),
                ).reshape(window + SUBLANES, lanes)
                turned.append(pltpu.roll(piece, col_rest, 1))
            for j in range(blocks + 1):
                if j == 0:
                    add = jnp.where(before, 0.0, turned[0])
                elif j == blocks:
                    add = jnp.where(before, turned[-1], 0.0)
                else:
                    add = jnp.where(before, turned[j - 1], turned[j])
                grad_ref[place(part, j)] += add
        return carry

    lax.fori_loop(0, count_ref[0], visit, 0)


def slot_gradients(count, offsets, extended, illumination, measured, dft):
    smem = pl.BlockSpec(memory_space=pltpu.SMEM)
    vmem = pl.BlockSpec(memory_space=pltpu.VMEM)
    return pl.pallas_call(
        compute_kernel,
        out_shape=(
            jax.ShapeDtypeStruct(extended.shape, jnp.float32),
            jax.ShapeDtypeStruct(illumination.shape, jnp.float32),
        ),
        in_specs=[smem, smem] + [vmem] * 7,
        out_specs=(vmem, vmem),
        compiler_params=pltpu.CompilerParams(vmem_limit_bytes=VMEM_LIMIT),
        name="slot_gradients",
    )(count, offsets, extended, illumination, measured, *dft)


def place_of():
    return lax.axis_index("ty"), lax.axis_index("tx"), lax.axis_size("ty"), lax.axis_size("tx")


def send_to(source, target, sems, index, row, col):
    send_sem, recv_sem = sems
    return pltpu.make_async_remote_copy(
        src_ref=source,
        dst_ref=target,
        send_sem=send_sem.at[index],
        recv_sem=recv_sem.at[index],
        device_id=(row, col),
        device_id_type=MESH,
    )


def wait_bytes(ref, sem):
    pltpu.make_async_copy(ref, ref, sem).wait()


def greet(partners):
    barrier = pltpu.get_barrier_semaphore()
    for exists, row, col in partners:
        @pl.when(exists)
        def _():
            pl.semaphore_signal(barrier, inc=1, device_id=(row, col), device_id_type=MESH)
    pl.semaphore_wait(barrier, sum(jnp.int32(exists) for exists, _, _ in partners))


def fetch_kernel(specimen, measured, reorder, reorder_t, extended, measured_out, send, recv, local):
    a, b, n_ty, n_tx = place_of()
    window = measured.shape[1]
    tile = specimen.shape[1]
    up, down, left, right = a > 0, a < n_ty - 1, b > 0, b < n_tx - 1
    greet([(up, a - 1, b), (down, a + 1, b), (left, a, b - 1), (right, a, b + 1)])
    sems = (send, recv)
    first, second = pl.ds(0, window), pl.ds(window, tile - window)
    beyond, inside = pl.ds(tile, window), pl.ds(0, tile)
    up_a = send_to(specimen.at[:, first, first], extended.at[:, beyond, first], sems, 0, a - 1, b)
    up_b = send_to(specimen.at[:, first, second], extended.at[:, beyond, second], sems, 1, a - 1, b)
    aside = send_to(specimen.at[:, :, first], extended.at[:, inside, beyond], sems, 2, a, b - 1)
    corner = send_to(extended.at[:, beyond, first], extended.at[:, beyond, beyond], sems, 3, a, b - 1)
    keep = pltpu.make_async_copy(specimen, extended.at[:, inside, inside], local)
    pl.when(up)(up_a.start)
    pl.when(left)(aside.start)
    keep.start()

    def rearrange(slot, carry):
        def pieces(value):
            high, low = split(value)
            rest = (value - high.astype(jnp.float32) - low.astype(jnp.float32)).astype(jnp.bfloat16)
            return [high, low, rest]

        rows = jnp.dot(
            reorder[...], jnp.concatenate(pieces(measured[slot]), axis=0),
            preferred_element_type=jnp.float32)
        measured_out[slot] = jnp.dot(
            jnp.concatenate(pieces(rows), axis=1), reorder_t[...],
            preferred_element_type=jnp.float32)
        return carry

    lax.fori_loop(0, measured.shape[0], rearrange, 0)

    @pl.when(up)
    def _():
        up_a.wait_send()
        up_b.start()

    @pl.when(down)
    def _():
        up_a.wait_recv()
        pl.when(left)(corner.start)

    keep.wait()
    pl.when(right)(aside.wait_recv)
    pl.when(left)(aside.wait_send)
    pl.when(up)(up_b.wait_send)
    pl.when(down)(up_b.wait_recv)
    pl.when(down & right)(corner.wait_recv)
    pl.when(down & left)(corner.wait_send)


def fetch(specimen, measured):
    window = measured.shape[1]
    side = specimen.shape[1] + window
    table = reorder_table(window)
    vmem = pl.BlockSpec(memory_space=pltpu.VMEM)
    hbm = pl.BlockSpec(memory_space=pl.ANY)
    return pl.pallas_call(
        fetch_kernel,
        out_shape=(
            jax.ShapeDtypeStruct((2, side, side), jnp.float32),
            jax.ShapeDtypeStruct(measured.shape, jnp.float32),
        ),
        in_specs=[hbm, vmem, vmem, vmem],
        out_specs=(hbm, vmem),
        scratch_shapes=[
            pltpu.SemaphoreType.DMA((4,)),
            pltpu.SemaphoreType.DMA((4,)),
            pltpu.SemaphoreType.DMA,
        ],
        compiler_params=pltpu.CompilerParams(
            collective_id=0, has_side_effects=True, vmem_limit_bytes=VMEM_LIMIT),
        name="fetch",
    )(specimen, measured, jnp.tile(table, (1, 3)), jnp.tile(table.T, (3, 1)))


class ProbeSum:
    def __init__(self, terms, buffers, send, recv):
        self.terms = terms
        self.mate, self.mine, self.pieces, self.strips, self.full, self.other = buffers
        self.send, self.recv = send, recv
        self.a, self.b, self.n_ty, n_tx = place_of()
        self.core = lax.rem(self.b, 2)
        self.pair = self.b // 2
        self.n_pair = n_tx // 2
        self.mate_col = self.b + 1 - 2 * self.core
        self.rows = self.full.shape[0] // self.n_ty

    @staticmethod
    def scratch(window, n_ty, n_tx):
        rows = window // n_ty
        return [
            pltpu.VMEM((window, window), jnp.float32),
            pltpu.VMEM((window, window), jnp.float32),
            pltpu.VMEM((n_ty - 1, rows, window), jnp.float32),
            pltpu.VMEM((n_tx // 2, rows, window), jnp.float32),
            pltpu.VMEM((window, window), jnp.float32),
            pltpu.VMEM((window, window), jnp.float32),
            pltpu.SemaphoreType.DMA((5,)),
            pltpu.SemaphoreType.DMA((5,)),
        ]

    def partners(self):
        found = [(True, self.a, self.mate_col)]
        found += [(True, lax.rem(self.a + d, self.n_ty), self.b) for d in range(1, self.n_ty)]
        found += [(True, self.a, 2 * lax.rem(self.pair + d, self.n_pair) + self.core) for d in range(1, self.n_pair)]
        return found

    def to(self, source, target, stage, row, col):
        return send_to(source, target, (self.send, self.recv), stage, row, col)

    def own(self, ref, row):
        return ref.at[pl.ds(pl.multiple_of(row * self.rows, SUBLANES), self.rows), :]

    def start(self):
        self.to(self.terms.at[1 - self.core], self.mate, 0, self.a, self.mate_col).start()

    def scatter(self):
        self.to(self.terms.at[1 - self.core], self.mate, 0, self.a, self.mate_col).wait()
        self.mine[...] = self.terms[self.core] + self.mate[...]

        def go(d, carry):
            row = lax.rem(self.a + d, self.n_ty)
            self.to(self.own(self.mine, row), self.pieces.at[d - 1], 1, row, self.b).start()
            return carry

        lax.fori_loop(1, self.n_ty, go, 0)

    def across(self):
        wait_bytes(self.pieces, self.recv.at[1])
        total = self.own(self.mine, self.a)[...]
        for d in range(self.n_ty - 1):
            total = total + self.pieces[d]
        self.strips[self.pair] = total

        def go(d, carry):
            col = 2 * lax.rem(self.pair + d, self.n_pair) + self.core
            self.to(self.strips.at[self.pair], self.strips.at[self.pair], 2, self.a, col).start()
            return carry

        lax.fori_loop(1, self.n_pair, go, 0)

    def gather(self):
        wait_bytes(self.strips.at[pl.ds(0, self.n_pair - 1)], self.recv.at[2])
        total = self.strips[0]
        for i in range(1, self.n_pair):
            total = total + self.strips[i]
        self.own(self.full, self.a)[...] = total

        def go(d, carry):
            row = lax.rem(self.a + d, self.n_ty)
            self.to(self.own(self.full, self.a), self.own(self.full, self.a), 3, row, self.b).start()
            return carry

        lax.fori_loop(1, self.n_ty, go, 0)

    def share(self):
        wait_bytes(self.full.at[pl.ds(0, (self.n_ty - 1) * self.rows)], self.recv.at[3])
        self.to(self.full, self.other, 4, self.a, self.mate_col).start()

    def finish(self, probe, probe_out):
        step = PROBE_GAIN / (POS_DEV * self.n_ty * 2 * self.n_pair)
        probe_out[self.core] = probe[self.core] - step * self.full[...]
        self.to(self.full, self.other, 4, self.a, self.mate_col).wait()
        probe_out[1 - self.core] = probe[1 - self.core] - step * self.other[...]
        wait_bytes(self.pieces, self.send.at[1])
        wait_bytes(self.strips.at[pl.ds(0, self.n_pair - 1)], self.send.at[2])
        wait_bytes(self.full.at[pl.ds(0, (self.n_ty - 1) * self.rows)], self.send.at[3])


def far_neighbour(a, b, n_tx):
    core = lax.rem(b, 2)
    col = b - 1 + 2 * core
    return ((col >= 0) & (col < n_tx), a, col)


def exchange_kernel(
    grad, extended, probe, probe_grad, extended_out, probe_out,
    gv, ev, from_left, from_right, from_up, from_down, send, recv, local,
    *probe_scratch,
):
    a, b, n_ty, n_tx = place_of()
    window = probe.shape[1]
    side = gv.shape[1]
    tile = side - window
    core = lax.rem(b, 2)
    has_up, has_down, has_left, has_right = a > 0, a < n_ty - 1, b > 0, b < n_tx - 1
    odd = core == 1
    total = ProbeSum(probe_grad, probe_scratch[:6], *probe_scratch[6:])
    greet(total.partners() + [far_neighbour(a, b, n_tx)])
    sems = (send, recv)
    start, middle, end = pl.ds(0, window), pl.ds(window, tile - window), pl.ds(tile, window)

    def across(rows, index):
        return (
            send_to(grad.at[:, rows, end], from_left.at[:, rows, :], sems, index, a, b + 1),
            send_to(grad.at[:, rows, start], from_right.at[:, rows, :], sems, index + 1, a, b - 1),
        )

    def along(source, cols, index):
        return (
            send_to(source.at[:, end, cols], from_up.at[:, :, cols], sems, index, a + 1, b),
            send_to(source.at[:, start, cols], from_down.at[:, :, cols], sems, index + 1, a - 1, b),
        )

    right_top, left_top = across(start, 0)
    right_mid, left_mid = across(middle, 2)
    right_end, left_end = across(end, 4)
    down_1, up_1 = along(grad, middle, 6)
    down_0, up_0 = along(gv, start, 8)
    down_2, up_2 = along(gv, end, 10)
    keep_top = send_to(ev.at[:, start, start], extended_out.at[:, start, end], sems, 12, a, b - 1)
    keep_end = send_to(ev.at[:, end, start], extended_out.at[:, end, end], sems, 13, a, b - 1)

    load_grad = pltpu.make_async_copy(grad, gv, local.at[0])
    load_extended = pltpu.make_async_copy(extended, ev, local.at[1])

    @pl.when(has_right)
    def _():
        right_top.start()
        right_end.start()

    @pl.when(has_left)
    def _():
        left_top.start()
        left_end.start()

    pl.when(has_down)(down_1.start)
    pl.when(has_up)(up_1.start)
    total.start()
    load_grad.start()
    load_extended.start()
    load_grad.wait()
    total.scatter()

    @pl.when(has_left)
    def _():
        right_top.wait_recv()
        right_end.wait_recv()
        gv[:, start, start] += from_left[:, start, :]
        gv[:, end, start] += from_left[:, end, :]

    @pl.when(has_down)
    def _():
        down_0.start()

    @pl.when(has_up)
    def _():
        up_0.start()

    @pl.when(has_right)
    def _():
        left_top.wait_recv()
        left_end.wait_recv()
        gv[:, start, end] += from_right[:, start, :]
        gv[:, end, end] += from_right[:, end, :]

    pl.when(has_down & odd)(down_2.start)
    pl.when(has_up & odd)(up_2.start)

    @pl.when(has_right)
    def _():
        right_top.wait_send()
        right_end.wait_send()
        right_mid.start()

    @pl.when(has_left)
    def _():
        left_top.wait_send()
        left_end.wait_send()
        left_mid.start()

    total.across()
    load_extended.wait()
    total.gather()

    @pl.when(has_left)
    def _():
        right_mid.wait_recv()
        gv[:, middle, start] += from_left[:, middle, :]

    @pl.when(has_right)
    def _():
        left_mid.wait_recv()
        gv[:, middle, end] += from_right[:, middle, :]

    ev[:, middle, :] -= OBJECT_STEP * gv[:, middle, :]
    store_mid = pltpu.make_async_copy(ev.at[:, middle, :], extended_out.at[:, middle, :], local.at[0])
    store_mid.start()
    total.share()

    def update(rows, cols, received, exists):
        @pl.when(exists)
        def _():
            ev[:, rows, cols] -= OBJECT_STEP * (gv[:, rows, cols] + received[:, :, cols])

        @pl.when(jnp.logical_not(exists))
        def _():
            ev[:, rows, cols] -= OBJECT_STEP * gv[:, rows, cols]

    pl.when(has_up)(down_0.wait_recv)
    pl.when(has_down)(up_0.wait_recv)
    update(start, start, from_up, has_up)
    update(end, start, from_down, has_down)

    @pl.when(odd)
    def _():
        keep_top.start()
        keep_end.start()

    pl.when(has_up)(down_1.wait_recv)
    pl.when(has_down)(up_1.wait_recv)
    update(start, middle, from_up, has_up)
    update(end, middle, from_down, has_down)
    inner = pl.ds(0, tile)
    store_top = pltpu.make_async_copy(ev.at[:, start, inner], extended_out.at[:, start, inner], local.at[1])
    store_end = pltpu.make_async_copy(ev.at[:, end, inner], extended_out.at[:, end, inner], local.at[2])
    store_top.start()
    store_end.start()

    @pl.when(odd)
    def _():
        pl.when(has_up)(down_2.wait_recv)
        pl.when(has_down)(up_2.wait_recv)
        update(start, end, from_up, has_up)
        update(end, end, from_down, has_down)
        rim_top = pltpu.make_async_copy(ev.at[:, start, end], extended_out.at[:, start, end], local.at[3])
        rim_end = pltpu.make_async_copy(ev.at[:, end, end], extended_out.at[:, end, end], local.at[4])
        rim_top.start()
        rim_end.start()
        rim_top.wait()
        rim_end.wait()
        keep_top.wait_send()
        keep_end.wait_send()

    total.finish(probe, probe_out)

    @pl.when(has_right)
    def _():
        right_mid.wait_send()

    @pl.when(has_left)
    def _():
        left_mid.wait_send()

    @pl.when(has_down)
    def _():
        down_0.wait_send()
        down_1.wait_send()
        pl.when(odd)(down_2.wait_send)

    @pl.when(has_up)
    def _():
        up_0.wait_send()
        up_1.wait_send()
        pl.when(odd)(up_2.wait_send)

    store_mid.wait()
    store_top.wait()
    store_end.wait()

    @pl.when(jnp.logical_not(odd))
    def _():
        keep_top.wait_recv()
        keep_end.wait_recv()


def exchange(grad, extended, illumination, probe_grad):
    window = illumination.shape[1]
    side = grad.shape[1]
    vmem = pl.BlockSpec(memory_space=pltpu.VMEM)
    hbm = pl.BlockSpec(memory_space=pl.ANY)
    return pl.pallas_call(
        exchange_kernel,
        out_shape=(
            jax.ShapeDtypeStruct(extended.shape, jnp.float32),
            jax.ShapeDtypeStruct(illumination.shape, jnp.float32),
        ),
        in_specs=[hbm, hbm, vmem, vmem],
        out_specs=(hbm, vmem),
        scratch_shapes=[
            pltpu.VMEM((2, side, side), jnp.float32),
            pltpu.VMEM((2, side, side), jnp.float32),
            pltpu.VMEM((2, side, window), jnp.float32),
            pltpu.VMEM((2, side, window), jnp.float32),
            pltpu.VMEM((2, window, side), jnp.float32),
            pltpu.VMEM((2, window, side), jnp.float32),
            pltpu.SemaphoreType.DMA((14,)),
            pltpu.SemaphoreType.DMA((14,)),
            pltpu.SemaphoreType.DMA((5,)),
        ] + ProbeSum.scratch(window, lax.axis_size("ty"), lax.axis_size("tx")),
        compiler_params=pltpu.CompilerParams(
            collective_id=1, has_side_effects=True, vmem_limit_bytes=VMEM_LIMIT),
        name="exchange",
    )(grad, extended, illumination, probe_grad)


def fold_kernel(
    grad, extended, probe, probe_grad, specimen_out, probe_out,
    gv, ev, corner, from_left, from_up, send, recv, local,
    *probe_scratch,
):
    a, b, n_ty, n_tx = place_of()
    window = probe.shape[1]
    side = gv.shape[1]
    tile = side - window
    has_up, has_down, has_left, has_right = a > 0, a < n_ty - 1, b > 0, b < n_tx - 1
    total = ProbeSum(probe_grad, probe_scratch[:6], *probe_scratch[6:])
    greet(total.partners() + [far_neighbour(a, b, n_tx)])
    sems = (send, recv)
    start, middle, end = pl.ds(0, window), pl.ds(window, tile - window), pl.ds(tile, window)
    inner = pl.ds(0, tile)
    right_end = send_to(grad.at[:, end, end], from_left.at[:, end, :], sems, 0, a, b + 1)
    right_rest = send_to(grad.at[:, inner, end], from_left.at[:, inner, :], sems, 1, a, b + 1)
    down_1 = send_to(grad.at[:, end, middle], from_up.at[:, :, middle], sems, 2, a + 1, b)
    down_0 = send_to(corner, from_up.at[:, :, start], sems, 3, a + 1, b)
    load_grad = pltpu.make_async_copy(grad.at[:, :, inner], gv, local.at[0])
    load_extended = pltpu.make_async_copy(extended.at[:, inner, inner], ev, local.at[1])
    pl.when(has_right)(right_end.start)
    pl.when(has_down)(down_1.start)
    total.start()
    load_grad.start()
    load_extended.start()
    total.scatter()
    load_grad.wait()

    @pl.when(has_left)
    def _():
        right_end.wait_recv()
        corner[...] = gv[:, end, start] + from_left[:, end, :]

    @pl.when(jnp.logical_not(has_left))
    def _():
        corner[...] = gv[:, end, start]

    pl.when(has_down)(down_0.start)

    @pl.when(has_right)
    def _():
        right_end.wait_send()
        right_rest.start()

    total.across()
    load_extended.wait()
    total.gather()
    ev[...] -= OBJECT_STEP * gv[:, inner, :]

    @pl.when(has_left)
    def _():
        right_rest.wait_recv()
        ev[:, :, start] -= OBJECT_STEP * from_left[:, inner, :]

    total.share()

    @pl.when(has_up)
    def _():
        down_1.wait_recv()
        down_0.wait_recv()
        ev[:, start, :] -= OBJECT_STEP * from_up[...]

    specimen_out[...] = ev[...]
    total.finish(probe, probe_out)
    pl.when(has_right)(right_rest.wait_send)

    @pl.when(has_down)
    def _():
        down_1.wait_send()
        down_0.wait_send()


def fold(grad, extended, illumination, probe_grad):
    window = illumination.shape[1]
    side = grad.shape[1]
    tile = side - window
    vmem = pl.BlockSpec(memory_space=pltpu.VMEM)
    hbm = pl.BlockSpec(memory_space=pl.ANY)
    return pl.pallas_call(
        fold_kernel,
        out_shape=(
            jax.ShapeDtypeStruct((2, tile, tile), jnp.float32),
            jax.ShapeDtypeStruct(illumination.shape, jnp.float32),
        ),
        in_specs=[hbm, hbm, vmem, vmem],
        out_specs=(vmem, vmem),
        scratch_shapes=[
            pltpu.VMEM((2, side, tile), jnp.float32),
            pltpu.VMEM((2, tile, tile), jnp.float32),
            pltpu.VMEM((2, window, window), jnp.float32),
            pltpu.VMEM((2, side, window), jnp.float32),
            pltpu.VMEM((2, window, tile), jnp.float32),
            pltpu.SemaphoreType.DMA((4,)),
            pltpu.SemaphoreType.DMA((4,)),
            pltpu.SemaphoreType.DMA((2,)),
        ] + ProbeSum.scratch(window, lax.axis_size("ty"), lax.axis_size("tx")),
        compiler_params=pltpu.CompilerParams(
            collective_id=2, has_side_effects=True, vmem_limit_bytes=VMEM_LIMIT),
        name="fold",
    )(grad, extended, illumination, probe_grad)


def body(specimen, illumination, patterns, scan_offsets, counts):
    window = illumination.shape[1]
    tile = specimen.shape[1]
    row_anchor = lax.axis_index("ty") * tile
    col_anchor = lax.axis_index("tx") * tile
    offsets = scan_offsets[0] - jnp.stack([row_anchor, col_anchor])[None, :].astype(jnp.int32)
    count = counts.reshape(1)
    dft = tables(window)
    extended, measured = fetch(specimen, patterns[0])
    for iteration in range(ITERS):
        grad, probe_grad = slot_gradients(count, offsets, extended, illumination, measured, dft)
        if iteration < ITERS - 1:
            extended, illumination = exchange(grad, extended, illumination, probe_grad)
        else:
            specimen, illumination = fold(grad, extended, illumination, probe_grad)
    return (specimen, illumination)


def solution(mesh):
    placed = (
        P(None, "ty", "tx"),
        P(),
        P("ty", "tx", None, None),
        P("ty", "tx", None),
        P("ty", "tx"),
    )
    return jax.shard_map(
        body, mesh=mesh, in_specs=placed, out_specs=(P(None, "ty", "tx"), P()), check_vma=False
    )
```

time: 1090 us -> 267 us (0.24); the launches traced: 1070 us -> 262 us
  waiting for transfers between devices: 659 us -> 0 us
  Pallas kernels: 0 us -> 254 us
  local copies, waits for them, and re-layouts: 158 us -> 6.53 us
  matrix products: 126 us -> 0 us
  other arithmetic: 47.6 us -> 0.08 us
  loops' own time: 47.2 us -> 0 us
  starting transfers between devices: 19.6 us -> 0 us
  between operations: 15.5 us -> 1.52 us
    psum x2 -> x0, waiting for transfers between devices: 491 us -> none  [body(): probe_total = lax.psum(probe_grad, ('ty', 'tx'))]
    pallas_call x0 -> x5, Pallas kernels: none -> 254 us  [the longest x1 105 us: exchange(): pl.pallas_call(exchange_kernel, out_shape=(jax.ShapeDtypeStruct(extended....]
    ppermute x8 -> x0, waiting for transfers between devices: 168 us -> none  [shifted(): lax.ppermute(value, axis, [(source, source + steps) for source in range(i...]
    dot_general x32 -> x0, matrix products: 126 us -> none  [the longest x16 63.5 us: apply_table(): return jnp.einsum('skn,nm->skm', batch, table, precision=HIGHEST)]
    dynamic_update_slice x12 -> x0, local copies, waits for them, and re-layouts: 77.4 us -> none  [add_slot(): lax.dynamic_update_slice(accum, current + object_terms[slot], (zero, corn...]
    another operation x4 -> x0, loops' own time: 47.2 us -> none  [the longest x2 46.7 us: slot_gradients(): lax.fori_loop(0, object_terms.shape[0], add_slot, jnp.zeros(extended.shap...]
    gather x36 -> x0, local copies, waits for them, and re-layouts: 43.9 us -> none
    ppermute x8 -> x0, starting transfers between devices: 19.6 us -> none  [shifted(): lax.ppermute(value, axis, [(source, source + steps) for source in range(i...]
  transfers between devices with their start and end apart: 10 -> 0, of which waited for: 8 -> 0; matrix products, arithmetic and copies ran while one was open for 1% -> 0% of each run, Pallas kernels for 0% -> 0%
where the time goes in v1:
time: 267 us; the launch traced here: 262 us
  Pallas kernels  254 us (95%)
  local copies, waits for them, and re-layouts  6.53 us (2%)
    pallas_call x1, Pallas kernels, exchange(): pl.pallas_call(exchange_kernel, out_shape=(jax.ShapeDtypeStruct(extended....  105 us
    pallas_call x1, Pallas kernels, fold(): pl.pallas_call(fold_kernel, out_shape=(jax.ShapeDtypeStruct((2, tile, til...  85.7 us
    pallas_call x1, Pallas kernels, fetch(): pl.pallas_call(fetch_kernel, out_shape=(jax.ShapeDtypeStruct((2, side, si...  38.6 us
    pallas_call x2, Pallas kernels, slot_gradients(): pl.pallas_call(compute_kernel, out_shape=(jax.ShapeDtypeStruct(extended.s...  24.6 us

profile of v1, /device:TPU:198, one launch (start us, length us, event | category | flops | bytes accessed | tf_op | source)
XLA Modules:
  0.0 261.9 jit_solution(8330696815448690689)
XLA Ops:
  0.6 0.0 copy-start.2
  1.4 0.1 pad_add_fusion
  1.5 0.8 copy.13
  2.3 0.9 tile.8
  3.2 0.2 copy.15.reorder
  3.4 0.9 tile.20
  4.3 0.0 copy-done.2
  4.3 0.0 copy-start
  4.3 1.6 copy-done
  5.9 0.0 copy-start.1
  5.9 0.0 copy-start.3
  5.9 0.0 copy-start.4
  5.9 0.0 copy-start.5
  5.9 0.0 copy-start.6
  5.9 38.6 %fetch.1 = (f32[2,768,768]{2,1,0:T(8,128)}, f32[6,256,256]{2,1,0:T(8,128)S(1)}) custom-call(f32[2,512,512]{2,1,0:T(8,128)S(1)} %copy-done, f32[6,256,256]{2,1,0:T(8,128)S(1)} %bitcast.9, bf16[256,768]{1,0:T(8,128)(2,1)S(1)} %copy.15.reorder, bf16[768,256]{1,0:T(8,128)(2,1)S(1)} %bitcast.10), custom_call_target="tpu_custom_call" | custom-call | tf_op jit(solution)/shard_map/fetch/pallas_call | solution.py:299
  44.6 0.0 copy-done.1
  44.6 0.0 copy-done.3
  44.6 0.0 copy-done.4
  44.6 0.0 copy-done.5
  44.6 0.0 copy-done.6
  44.6 12.3 %slot_gradients.2 = (f32[2,768,768]{2,1,0:T(8,128)}, f32[2,256,256]{2,1,0:T(8,128)S(1)}) custom-call(s32[1]{0:T(128)} %bitcast.7.count_ref, s32[6,2]{1,0:T(8,128)S(1)} %broadcast_subtract_fusion.offsets_ref, f32[2,768,768]{2,1,0:T(8,128)} %get-tuple-element.10.specimen_ref.extended, f32[2,256,256]{2,1,0:T(8,128)S(1)} %copy-done.1, ...), custom_call_target="tpu_custom_call" | custom-call | tf_op jit(solution)/shard_map/slot_gradients/pallas_call | solution.py:198
  57.0 104.9 %exchange.1 = (f32[2,768,768]{2,1,0:T(8,128)}, f32[2,256,256]{2,1,0:T(8,128)S(1)}) custom-call(f32[2,768,768]{2,1,0:T(8,128)} %get-tuple-element.12.grad, f32[2,768,768]{2,1,0:T(8,128)} %get-tuple-element.10.specimen_ref.extended, f32[2,256,256]{2,1,0:T(8,128)S(1)} %copy-done.1, f32[2,256,256]{2,1,0:T(8,128)S(1)} %get-tuple-element.13.probe_grad), custom_call_target="tpu_custom_call" | custom-call | tf_op jit(solution)/shard_map/exchange/pallas_call | solution.py:614
  161.9 12.2 %slot_gradients.3 = (f32[2,768,768]{2,1,0:T(8,128)}, f32[2,256,256]{2,1,0:T(8,128)S(1)}) custom-call(s32[1]{0:T(128)} %bitcast.8.count_ref, s32[6,2]{1,0:T(8,128)S(1)} %broadcast_subtract_fusion.offsets_ref, f32[2,768,768]{2,1,0:T(8,128)} %get-tuple-element.14.specimen_ref.extended, f32[2,256,256]{2,1,0:T(8,128)S(1)} %get-tuple-element.15.probe_ref.probe, ...), custom_call_target="tpu_custom_call" | custom-call | tf_op jit(solution)/shard_map/slot_gradients/pallas_call | solution.py:198
  174.1 85.7 %fold.1 = (f32[2,512,512]{2,1,0:T(8,128)S(1)}, f32[2,256,256]{2,1,0:T(8,128)S(1)}) custom-call(f32[2,768,768]{2,1,0:T(8,128)} %get-tuple-element.16.grad, f32[2,768,768]{2,1,0:T(8,128)} %get-tuple-element.14.specimen_ref.extended, f32[2,256,256]{2,1,0:T(8,128)S(1)} %get-tuple-element.15.probe_ref.probe, f32[2,256,256]{2,1,0:T(8,128)S(1)} %get-tuple-element.17.probe_grad), custom_call_target="tpu_custom_call" | custom-call | tf_op jit(solution)/shard_map/fold/pallas_call | solution.py:718
  259.8 1.3 copy.19
  261.1 0.8 copy.20
  (1 shorter events, 0.0 us)
Async XLA Ops:
  0.6 3.7 %copy-start.2 = (f32[1,6,256,256]{3,2,1,0:T(8,128)S(1)}, f32[1,6,256,256]{3,2,1,0:T(8,128)}, u32[]{:S(2)}) copy-start(f32[1,6,256,256]{3,2,1,0:T(8,128)} %param.12) | copy-start | bytes 4718596
  4.3 1.6 copy-start
  5.9 38.7 %copy-start.1 = (f32[2,256,256]{2,1,0:T(8,128)S(1)}, f32[2,256,256]{2,1,0:T(8,128)}, u32[]{:S(2)}) copy-start(f32[2,256,256]{2,1,0:T(8,128)} %probe.1) | copy-start | bytes 1572868
  5.9 38.7 %copy-start.3 = (bf16[768,256]{1,0:T(8,128)(2,1)S(1)}, bf16[768,256]{1,0:T(8,128)(2,1)}, u32[]{:S(2)}) copy-start(bf16[768,256]{1,0:T(8,128)(2,1)} %constant.22.clone.right_back_ref) | copy-start | bytes 1179652
  5.9 38.7 %copy-start.4 = (bf16[256,768]{1,0:T(8,128)(2,1)S(1)}, bf16[256,768]{1,0:T(8,128)(2,1)}, u32[]{:S(2)}) copy-start(bf16[256,768]{1,0:T(8,128)(2,1)} %constant.21.clone.left_back_ref) | copy-start | bytes 1179652
  5.9 38.7 %copy-start.5 = (bf16[768,256]{1,0:T(8,128)(2,1)S(1)}, bf16[768,256]{1,0:T(8,128)(2,1)}, u32[]{:S(2)}) copy-start(bf16[768,256]{1,0:T(8,128)(2,1)} %constant.20.clone.right_ref) | copy-start | bytes 1179652
  5.9 38.7 %copy-start.6 = (bf16[256,768]{1,0:T(8,128)(2,1)S(1)}, bf16[256,768]{1,0:T(8,128)(2,1)}, u32[]{:S(2)}) copy-start(bf16[256,768]{1,0:T(8,128)(2,1)} %constant.19.clone.left_ref) | copy-start | bytes 1179652

commit v2 on v1

--- a/solution.py
+++ b/solution.py
@@ -46,7 +46,7 @@
     half = window // 2
     i = np.arange(window)
     freq = np.where(i <= half, i, window + half - i)
-    return jnp.asarray((freq[:, None] == i[None, :]).astype(ml_dtypes.bfloat16))
+    return (freq[:, None] == i[None, :]).astype(ml_dtypes.bfloat16)
 
 
 def split(value):
@@ -237,23 +237,162 @@
     pl.semaphore_wait(barrier, sum(jnp.int32(exists) for exists, _, _ in partners))
 
 
-def fetch_kernel(specimen, measured, reorder, reorder_t, extended, measured_out, send, recv, local):
+class Boundary:
+    def __init__(self, relay, sems):
+        self.relay = relay
+        self.hop_send, self.hop_recv, self.end_send, self.end_recv = sems
+        self.a, self.b, _, self.n_tx = place_of()
+        self.low = self.n_tx // 2 - 1
+        self.at_low, self.at_high = self.b == self.low, self.b == self.low + 1
+
+    @staticmethod
+    def scratch(window):
+        return [
+            pltpu.VMEM((2, 3, window, window), jnp.float32),
+            pltpu.SemaphoreType.DMA((2, 3, 2)),
+            pltpu.SemaphoreType.DMA((2, 3)),
+            pltpu.SemaphoreType.DMA((2, 3)),
+            pltpu.SemaphoreType.DMA((2, 3, 2)),
+        ]
+
+    def partner(self):
+        last = self.n_tx - 1
+        col = jnp.where(
+            self.b == 0, self.low, jnp.where(
+                self.at_low, 0, jnp.where(self.at_high, last, self.low + 1)))
+        exists = (self.b == 0) | (self.b == last) | self.at_low | self.at_high
+        return (exists, self.a, col)
+
+    def origin(self, way):
+        return self.low if way == 0 else self.low + 1
+
+    def stop(self, part):
+        return 0 if part == 0 else self.n_tx - 1
+
+    def first(self, way, index, part, source):
+        return pltpu.make_async_remote_copy(
+            src_ref=source.at[part],
+            dst_ref=self.relay.at[way, index],
+            send_sem=self.hop_send.at[way, index, part],
+            recv_sem=self.hop_recv.at[way, index],
+            device_id=(self.a, self.stop(part)),
+            device_id_type=MESH,
+        )
+
+    def second(self, way, index, part, target):
+        return pltpu.make_async_remote_copy(
+            src_ref=self.relay.at[way, index],
+            dst_ref=target.at[part],
+            send_sem=self.end_send.at[way, index],
+            recv_sem=self.end_recv.at[way, index, part],
+            device_id=(self.a, self.origin(1 - way)),
+            device_id_type=MESH,
+        )
+
+    def start(self, way, index, source):
+        for part in range(2):
+            self.first(way, index, part, source).start()
+
+    def pass_on(self, way, index, source, target):
+        for part in range(2):
+            @pl.when(self.b == self.stop(part))
+            def _():
+                self.first(way, index, part, source).wait_recv()
+                self.second(way, index, part, target).start()
+
+    def passed(self, way, index, target):
+        for part in range(2):
+            @pl.when(self.b == self.stop(part))
+            def _():
+                self.second(way, index, part, target).wait_send()
+
+    def wait_recv(self, way, index, target):
+        for part in range(2):
+            self.second(way, index, part, target).wait_recv()
+
+    def wait_send(self, way, index, source):
+        for part in range(2):
+            self.first(way, index, part, source).wait_send()
+
+
+class Sideways:
+    def __init__(self, boundary, way, index, source, target, sems, slot):
+        a, b, _, n_tx = place_of()
+        self.boundary, self.way, self.index = boundary, way, index
+        self.source, self.target = source, target
+        step = 1 if way == 0 else -1
+        self.direct = send_to(source, target, sems, slot, a, b + step)
+        left, right = b > 0, b < n_tx - 1
+        self.has_target, self.has_source = (right, left) if way == 0 else (left, right)
+        self.from_origin = b == boundary.origin(way)
+        self.at_end = b == boundary.origin(1 - way)
+
+    def start(self):
+        pl.when(self.from_origin)(lambda: self.boundary.start(self.way, self.index, self.source))
+        pl.when(self.has_target & ~self.from_origin)(self.direct.start)
+
+    def pass_on(self):
+        self.boundary.pass_on(self.way, self.index, self.source, self.target)
+
+    def wait_recv(self):
+        pl.when(self.at_end)(lambda: self.boundary.wait_recv(self.way, self.index, self.target))
+        pl.when(self.has_source & ~self.at_end)(self.direct.wait_recv)
+
+    def wait_send(self):
+        pl.when(self.from_origin)(lambda: self.boundary.wait_send(self.way, self.index, self.source))
+        pl.when(self.has_target & ~self.from_origin)(self.direct.wait_send)
+
+    def passed(self):
+        self.boundary.passed(self.way, self.index, self.target)
+
+
+def fetch_kernel(
+    specimen, patterns, reorder, reorder_t, extended, measured_out,
+    measured, send, recv, local, *boundary_scratch,
+):
     a, b, n_ty, n_tx = place_of()
     window = measured.shape[1]
     tile = specimen.shape[1]
     up, down, left, right = a > 0, a < n_ty - 1, b > 0, b < n_tx - 1
-    greet([(up, a - 1, b), (down, a + 1, b), (left, a, b - 1), (right, a, b + 1)])
+    boundary = Boundary(boundary_scratch[0], boundary_scratch[1:])
+    near = (True, a, b + 1 - 2 * lax.rem(b, 2))
+    relays = [(b == 0, a, boundary.low + 1), (boundary.at_high, a, 0)]
+    relays += [(b == n_tx - 1, a, boundary.low), (boundary.at_low, a, n_tx - 1)]
+    greet([(up, a - 1, b), (down, a + 1, b), near, far_neighbour(a, b, n_tx), boundary.partner()] + relays)
     sems = (send, recv)
     first, second = pl.ds(0, window), pl.ds(window, tile - window)
     beyond, inside = pl.ds(tile, window), pl.ds(0, tile)
     up_a = send_to(specimen.at[:, first, first], extended.at[:, beyond, first], sems, 0, a - 1, b)
     up_b = send_to(specimen.at[:, first, second], extended.at[:, beyond, second], sems, 1, a - 1, b)
-    aside = send_to(specimen.at[:, :, first], extended.at[:, inside, beyond], sems, 2, a, b - 1)
-    corner = send_to(extended.at[:, beyond, first], extended.at[:, beyond, beyond], sems, 3, a, b - 1)
-    keep = pltpu.make_async_copy(specimen, extended.at[:, inside, inside], local)
+
+    def aside(index, source, rows):
+        return Sideways(
+            boundary, 1, index, source.at[:, rows, first], extended.at[:, rows, beyond], sems, 2 + index)
+
+    aside_a = aside(0, specimen, first)
+    aside_b = aside(1, specimen, second)
+    corner = aside(2, extended, beyond)
+    keep = pltpu.make_async_copy(specimen, extended.at[:, inside, inside], local.at[0])
+    load = pltpu.make_async_copy(patterns.at[0], measured, local.at[1])
     pl.when(up)(up_a.start)
-    pl.when(left)(aside.start)
+    aside_a.start()
+    aside_b.start()
+    load.start()
     keep.start()
+    aside_a.pass_on()
+    aside_b.pass_on()
+
+    @pl.when(up)
+    def _():
+        up_a.wait_send()
+        up_b.start()
+
+    @pl.when(down)
+    def _():
+        up_a.wait_recv()
+        corner.start()
+
+    load.wait()
 
     def rearrange(slot, carry):
         def pieces(value):
@@ -270,28 +409,29 @@
         return carry
 
     lax.fori_loop(0, measured.shape[0], rearrange, 0)
+    pl.when(down)(corner.pass_on)
+    keep.wait()
+    aside_a.wait_recv()
+    aside_b.wait_recv()
 
     @pl.when(up)
     def _():
-        up_a.wait_send()
-        up_b.start()
+        up_b.wait_send()
 
     @pl.when(down)
     def _():
-        up_a.wait_recv()
-        pl.when(left)(corner.start)
-
-    keep.wait()
-    pl.when(right)(aside.wait_recv)
-    pl.when(left)(aside.wait_send)
-    pl.when(up)(up_b.wait_send)
-    pl.when(down)(up_b.wait_recv)
-    pl.when(down & right)(corner.wait_recv)
-    pl.when(down & left)(corner.wait_send)
-
-
-def fetch(specimen, measured):
-    window = measured.shape[1]
+        up_b.wait_recv()
+        corner.wait_recv()
+        corner.wait_send()
+        corner.passed()
+
+    for strip in (aside_a, aside_b):
+        strip.wait_send()
+        strip.passed()
+
+
+def fetch(specimen, patterns):
+    window = patterns.shape[2]
     side = specimen.shape[1] + window
     table = reorder_table(window)
     vmem = pl.BlockSpec(memory_space=pltpu.VMEM)
@@ -300,19 +440,20 @@
         fetch_kernel,
         out_shape=(
             jax.ShapeDtypeStruct((2, side, side), jnp.float32),
-            jax.ShapeDtypeStruct(measured.shape, jnp.float32),
+            jax.ShapeDtypeStruct(patterns.shape[1:], jnp.float32),
         ),
-        in_specs=[hbm, vmem, vmem, vmem],
+        in_specs=[hbm, hbm, vmem, vmem],
         out_specs=(hbm, vmem),
         scratch_shapes=[
-            pltpu.SemaphoreType.DMA((4,)),
-            pltpu.SemaphoreType.DMA((4,)),
-            pltpu.SemaphoreType.DMA,
-        ],
+            pltpu.VMEM(patterns.shape[1:], jnp.float32),
+            pltpu.SemaphoreType.DMA((5,)),
+            pltpu.SemaphoreType.DMA((5,)),
+            pltpu.SemaphoreType.DMA((2,)),
+        ] + Boundary.scratch(window),
         compiler_params=pltpu.CompilerParams(
             collective_id=0, has_side_effects=True, vmem_limit_bytes=VMEM_LIMIT),
         name="fetch",
-    )(specimen, measured, jnp.tile(table, (1, 3)), jnp.tile(table.T, (3, 1)))
+    )(specimen, patterns, jnp.asarray(np.tile(table, (1, 3))), jnp.asarray(np.tile(table.T, (3, 1))))
 
 
 class ProbeSum:
@@ -412,13 +553,13 @@
 def far_neighbour(a, b, n_tx):
     core = lax.rem(b, 2)
     col = b - 1 + 2 * core
-    return ((col >= 0) & (col < n_tx), a, col)
+    return ((col >= 0) & (col < n_tx) & (b != n_tx // 2 - 1) & (b != n_tx // 2), a, col)
 
 
 def exchange_kernel(
     grad, extended, probe, probe_grad, extended_out, probe_out,
     gv, ev, from_left, from_right, from_up, from_down, send, recv, local,
-    *probe_scratch,
+    *rest,
 ):
     a, b, n_ty, n_tx = place_of()
     window = probe.shape[1]
@@ -427,15 +568,16 @@
     core = lax.rem(b, 2)
     has_up, has_down, has_left, has_right = a > 0, a < n_ty - 1, b > 0, b < n_tx - 1
     odd = core == 1
-    total = ProbeSum(probe_grad, probe_scratch[:6], *probe_scratch[6:])
-    greet(total.partners() + [far_neighbour(a, b, n_tx)])
+    total = ProbeSum(probe_grad, rest[:6], *rest[6:8])
+    boundary = Boundary(rest[8], rest[9:])
+    greet(total.partners() + [far_neighbour(a, b, n_tx), boundary.partner()])
     sems = (send, recv)
     start, middle, end = pl.ds(0, window), pl.ds(window, tile - window), pl.ds(tile, window)
 
     def across(rows, index):
         return (
-            send_to(grad.at[:, rows, end], from_left.at[:, rows, :], sems, index, a, b + 1),
-            send_to(grad.at[:, rows, start], from_right.at[:, rows, :], sems, index + 1, a, b - 1),
+            Sideways(boundary, 0, index, grad.at[:, rows, end], from_left.at[:, rows, :], sems, 2 * index),
+            Sideways(boundary, 1, index, grad.at[:, rows, start], from_right.at[:, rows, :], sems, 2 * index + 1),
         )
 
     def along(source, cols, index):
@@ -445,8 +587,8 @@
         )
 
     right_top, left_top = across(start, 0)
+    right_end, left_end = across(end, 1)
     right_mid, left_mid = across(middle, 2)
-    right_end, left_end = across(end, 4)
     down_1, up_1 = along(grad, middle, 6)
     down_0, up_0 = along(gv, start, 8)
     down_2, up_2 = along(gv, end, 10)
@@ -456,79 +598,64 @@
     load_grad = pltpu.make_async_copy(grad, gv, local.at[0])
     load_extended = pltpu.make_async_copy(extended, ev, local.at[1])
 
-    @pl.when(has_right)
-    def _():
-        right_top.start()
-        right_end.start()
-
-    @pl.when(has_left)
-    def _():
-        left_top.start()
-        left_end.start()
-
+    outer = (right_top, right_end, left_top, left_end)
+    for strip in outer:
+        strip.start()
     pl.when(has_down)(down_1.start)
     pl.when(has_up)(up_1.start)
     total.start()
     load_grad.start()
     load_extended.start()
+    total.scatter()
+    right_top.pass_on()
+    right_end.pass_on()
+    total.across()
+    left_top.pass_on()
+    left_end.pass_on()
+    total.gather()
     load_grad.wait()
-    total.scatter()
+    right_top.wait_recv()
+    right_end.wait_recv()
 
     @pl.when(has_left)
     def _():
-        right_top.wait_recv()
-        right_end.wait_recv()
         gv[:, start, start] += from_left[:, start, :]
         gv[:, end, start] += from_left[:, end, :]
 
-    @pl.when(has_down)
-    def _():
-        down_0.start()
-
-    @pl.when(has_up)
-    def _():
-        up_0.start()
+    pl.when(has_down)(down_0.start)
+    pl.when(has_up)(up_0.start)
+    left_top.wait_recv()
+    left_end.wait_recv()
 
     @pl.when(has_right)
     def _():
-        left_top.wait_recv()
-        left_end.wait_recv()
         gv[:, start, end] += from_right[:, start, :]
         gv[:, end, end] += from_right[:, end, :]
 
     pl.when(has_down & odd)(down_2.start)
     pl.when(has_up & odd)(up_2.start)
+    for strip in outer:
+        strip.wait_send()
+    right_mid.start()
+    left_mid.start()
+    right_mid.pass_on()
+    left_mid.pass_on()
+    total.share()
+    load_extended.wait()
+    right_mid.wait_recv()
+    left_mid.wait_recv()
+
+    @pl.when(has_left)
+    def _():
+        gv[:, middle, start] += from_left[:, middle, :]
 
     @pl.when(has_right)
     def _():
-        right_top.wait_send()
-        right_end.wait_send()
-        right_mid.start()
-
-    @pl.when(has_left)
-    def _():
-        left_top.wait_send()
-        left_end.wait_send()
-        left_mid.start()
-
-    total.across()
-    load_extended.wait()
-    total.gather()
-
-    @pl.when(has_left)
-    def _():
-        right_mid.wait_recv()
-        gv[:, middle, start] += from_left[:, middle, :]
-
-    @pl.when(has_right)
-    def _():
-        left_mid.wait_recv()
         gv[:, middle, end] += from_right[:, middle, :]
 
     ev[:, middle, :] -= OBJECT_STEP * gv[:, middle, :]
     store_mid = pltpu.make_async_copy(ev.at[:, middle, :], extended_out.at[:, middle, :], local.at[0])
     store_mid.start()
-    total.share()
 
     def update(rows, cols, received, exists):
         @pl.when(exists)
@@ -575,14 +702,10 @@
         keep_end.wait_send()
 
     total.finish(probe, probe_out)
-
-    @pl.when(has_right)
-    def _():
-        right_mid.wait_send()
-
-    @pl.when(has_left)
-    def _():
-        left_mid.wait_send()
+    right_mid.wait_send()
+    left_mid.wait_send()
+    for strip in outer + (right_mid, left_mid):
+        strip.passed()
 
     @pl.when(has_down)
     def _():
@@ -629,7 +752,7 @@
             pltpu.SemaphoreType.DMA((14,)),
             pltpu.SemaphoreType.DMA((14,)),
             pltpu.SemaphoreType.DMA((5,)),
-        ] + ProbeSum.scratch(window, lax.axis_size("ty"), lax.axis_size("tx")),
+        ] + ProbeSum.scratch(window, lax.axis_size("ty"), lax.axis_size("tx")) + Boundary.scratch(window),
         compiler_params=pltpu.CompilerParams(
             collective_id=1, has_side_effects=True, vmem_limit_bytes=VMEM_LIMIT),
         name="exchange",
@@ -639,35 +762,43 @@
 def fold_kernel(
     grad, extended, probe, probe_grad, specimen_out, probe_out,
     gv, ev, corner, from_left, from_up, send, recv, local,
-    *probe_scratch,
+    *rest,
 ):
     a, b, n_ty, n_tx = place_of()
     window = probe.shape[1]
     side = gv.shape[1]
     tile = side - window
     has_up, has_down, has_left, has_right = a > 0, a < n_ty - 1, b > 0, b < n_tx - 1
-    total = ProbeSum(probe_grad, probe_scratch[:6], *probe_scratch[6:])
-    greet(total.partners() + [far_neighbour(a, b, n_tx)])
+    total = ProbeSum(probe_grad, rest[:6], *rest[6:8])
+    boundary = Boundary(rest[8], rest[9:])
+    greet(total.partners() + [far_neighbour(a, b, n_tx), boundary.partner()])
     sems = (send, recv)
     start, middle, end = pl.ds(0, window), pl.ds(window, tile - window), pl.ds(tile, window)
     inner = pl.ds(0, tile)
-    right_end = send_to(grad.at[:, end, end], from_left.at[:, end, :], sems, 0, a, b + 1)
-    right_rest = send_to(grad.at[:, inner, end], from_left.at[:, inner, :], sems, 1, a, b + 1)
-    down_1 = send_to(grad.at[:, end, middle], from_up.at[:, :, middle], sems, 2, a + 1, b)
-    down_0 = send_to(corner, from_up.at[:, :, start], sems, 3, a + 1, b)
+
+    def across(rows, index):
+        return Sideways(boundary, 0, index, grad.at[:, rows, end], from_left.at[:, rows, :], sems, index)
+
+    right_end = across(end, 0)
+    right_top = across(start, 1)
+    right_mid = across(middle, 2)
+    down_1 = send_to(grad.at[:, end, middle], from_up.at[:, :, middle], sems, 3, a + 1, b)
+    down_0 = send_to(corner, from_up.at[:, :, start], sems, 4, a + 1, b)
     load_grad = pltpu.make_async_copy(grad.at[:, :, inner], gv, local.at[0])
     load_extended = pltpu.make_async_copy(extended.at[:, inner, inner], ev, local.at[1])
-    pl.when(has_right)(right_end.start)
+    right_end.start()
     pl.when(has_down)(down_1.start)
     total.start()
     load_grad.start()
     load_extended.start()
     total.scatter()
+    right_end.pass_on()
+    total.across()
     load_grad.wait()
+    right_end.wait_recv()
 
     @pl.when(has_left)
     def _():
-        right_end.wait_recv()
         corner[...] = gv[:, end, start] + from_left[:, end, :]
 
     @pl.when(jnp.logical_not(has_left))
@@ -675,23 +806,21 @@
         corner[...] = gv[:, end, start]
 
     pl.when(has_down)(down_0.start)
-
-    @pl.when(has_right)
-    def _():
-        right_end.wait_send()
-        right_rest.start()
-
-    total.across()
+    right_end.wait_send()
+    right_top.start()
+    right_mid.start()
+    total.gather()
+    right_top.pass_on()
+    right_mid.pass_on()
     load_extended.wait()
-    total.gather()
     ev[...] -= OBJECT_STEP * gv[:, inner, :]
+    total.share()
+    right_top.wait_recv()
+    right_mid.wait_recv()
 
     @pl.when(has_left)
     def _():
-        right_rest.wait_recv()
         ev[:, :, start] -= OBJECT_STEP * from_left[:, inner, :]
-
-    total.share()
 
     @pl.when(has_up)
     def _():
@@ -701,7 +830,10 @@
 
     specimen_out[...] = ev[...]
     total.finish(probe, probe_out)
-    pl.when(has_right)(right_rest.wait_send)
+    right_top.wait_send()
+    right_mid.wait_send()
+    for strip in (right_end, right_top, right_mid):
+        strip.passed()
 
     @pl.when(has_down)
     def _():
@@ -729,10 +861,10 @@
             pltpu.VMEM((2, window, window), jnp.float32),
             pltpu.VMEM((2, side, window), jnp.float32),
             pltpu.VMEM((2, window, tile), jnp.float32),
-            pltpu.SemaphoreType.DMA((4,)),
-            pltpu.SemaphoreType.DMA((4,)),
+            pltpu.SemaphoreType.DMA((5,)),
+            pltpu.SemaphoreType.DMA((5,)),
             pltpu.SemaphoreType.DMA((2,)),
-        ] + ProbeSum.scratch(window, lax.axis_size("ty"), lax.axis_size("tx")),
+        ] + ProbeSum.scratch(window, lax.axis_size("ty"), lax.axis_size("tx")) + Boundary.scratch(window),
         compiler_params=pltpu.CompilerParams(
             collective_id=2, has_side_effects=True, vmem_limit_bytes=VMEM_LIMIT),
         name="fold",
@@ -747,7 +879,7 @@
     offsets = scan_offsets[0] - jnp.stack([row_anchor, col_anchor])[None, :].astype(jnp.int32)
     count = counts.reshape(1)
     dft = tables(window)
-    extended, measured = fetch(specimen, patterns[0])
+    extended, measured = fetch(specimen, patterns)
     for iteration in range(ITERS):
         grad, probe_grad = slot_gradients(count, offsets, extended, illumination, measured, dft)
         if iteration < ITERS - 1:

time: 267 us -> 228 us (0.85); the launches traced: 262 us -> 228 us
  Pallas kernels: 254 us -> 219 us
    pallas_call x1, Pallas kernels: 105 us -> 86 us  [exchange(): pl.pallas_call(exchange_kernel, out_shape=(jax.ShapeDtypeStruct(extended....]
    pallas_call x1, Pallas kernels: 85.7 us -> 74.8 us  [fold(): pl.pallas_call(fold_kernel, out_shape=(jax.ShapeDtypeStruct((2, tile, til...]
    pallas_call x1, Pallas kernels: 38.6 us -> 33.3 us  [fetch(): pl.pallas_call(fetch_kernel, out_shape=(jax.ShapeDtypeStruct((2, side, si...]
    unnamed x16 -> x20, local copies, waits for them, and re-layouts: 3.73 us -> 7.12 us
where the time goes in v2:
time: 228 us
  Pallas kernels  219 us (96%)
  local copies, waits for them, and re-layouts  7.89 us (3%)
    pallas_call x1, Pallas kernels, exchange(): pl.pallas_call(exchange_kernel, out_shape=(jax.ShapeDtypeStruct(extended....  86 us
    pallas_call x1, Pallas kernels, fold(): pl.pallas_call(fold_kernel, out_shape=(jax.ShapeDtypeStruct((2, tile, til...  74.8 us
    pallas_call x1, Pallas kernels, fetch(): pl.pallas_call(fetch_kernel, out_shape=(jax.ShapeDtypeStruct((2, side, si...  33.3 us
    pallas_call x2, Pallas kernels, slot_gradients(): pl.pallas_call(compute_kernel, out_shape=(jax.ShapeDtypeStruct(extended.s...  24.4 us
    unnamed x20, local copies, waits for them, and re-layouts  7.12 us

profile of v2, /device:TPU:198, one launch (start us, length us, event | category | flops | bytes accessed | tf_op | source)
XLA Modules:
  0.0 227.9 jit_solution(13069365901301127010)
XLA Ops:
  1.3 0.1 pad_add_fusion
  1.4 0.8 copy.13
  2.1 0.0 copy-start
  2.1 1.6 copy-done
  3.7 0.0 copy-start.2
  3.7 1.4 copy-done.2
  5.1 0.0 copy-start.7
  5.1 1.0 copy-done.7
  6.1 0.0 copy-start.8
  6.1 1.0 copy-done.8
  7.1 0.0 copy-start.1
  7.1 0.0 copy-start.3
  7.1 0.0 copy-start.4
  7.1 0.0 copy-start.5
  7.1 0.0 copy-start.6
  7.1 33.3 %fetch.1 = (f32[2,768,768]{2,1,0:T(8,128)}, f32[6,256,256]{2,1,0:T(8,128)S(1)}) custom-call(f32[2,512,512]{2,1,0:T(8,128)S(1)} %copy-done, f32[1,6,256,256]{3,2,1,0:T(8,128)S(1)} %copy-done.2, bf16[256,768]{1,0:T(8,128)(2,1)S(1)} %copy-done.8, bf16[768,256]{1,0:T(8,128)(2,1)S(1)} %copy-done.7), custom_call_target="tpu_custom_call" | custom-call | tf_op jit(solution)/shard_map/fetch/pallas_call | solution.py:439
  40.5 0.0 copy-done.1
  40.5 0.0 copy-done.3
  40.5 0.0 copy-done.4
  40.5 0.0 copy-done.5
  40.5 0.0 copy-done.6
  40.5 12.2 %slot_gradients.2 = (f32[2,768,768]{2,1,0:T(8,128)}, f32[2,256,256]{2,1,0:T(8,128)S(1)}) custom-call(s32[1]{0:T(128)} %bitcast.4.count_ref, s32[6,2]{1,0:T(8,128)S(1)} %broadcast_subtract_fusion.offsets_ref, f32[2,768,768]{2,1,0:T(8,128)} %get-tuple-element.10.specimen_ref.extended, f32[2,256,256]{2,1,0:T(8,128)S(1)} %copy-done.1, ...), custom_call_target="tpu_custom_call" | custom-call | tf_op jit(solution)/shard_map/slot_gradients/pallas_call | solution.py:198
  52.8 86.0 %exchange.1 = (f32[2,768,768]{2,1,0:T(8,128)}, f32[2,256,256]{2,1,0:T(8,128)S(1)}) custom-call(f32[2,768,768]{2,1,0:T(8,128)} %get-tuple-element.12.grad, f32[2,768,768]{2,1,0:T(8,128)} %get-tuple-element.10.specimen_ref.extended, f32[2,256,256]{2,1,0:T(8,128)S(1)} %copy-done.1, f32[2,256,256]{2,1,0:T(8,128)S(1)} %get-tuple-element.13.probe_grad), custom_call_target="tpu_custom_call" | custom-call | tf_op jit(solution)/shard_map/exchange/pallas_call | solution.py:737
  138.8 12.2 %slot_gradients.3 = (f32[2,768,768]{2,1,0:T(8,128)}, f32[2,256,256]{2,1,0:T(8,128)S(1)}) custom-call(s32[1]{0:T(128)} %bitcast.5.count_ref, s32[6,2]{1,0:T(8,128)S(1)} %broadcast_subtract_fusion.offsets_ref, f32[2,768,768]{2,1,0:T(8,128)} %get-tuple-element.14.specimen_ref.extended, f32[2,256,256]{2,1,0:T(8,128)S(1)} %get-tuple-element.15.probe_ref.probe, ...), custom_call_target="tpu_custom_call" | custom-call | tf_op jit(solution)/shard_map/slot_gradients/pallas_call | solution.py:198
  151.0 74.8 %fold.1 = (f32[2,512,512]{2,1,0:T(8,128)S(1)}, f32[2,256,256]{2,1,0:T(8,128)S(1)}) custom-call(f32[2,768,768]{2,1,0:T(8,128)} %get-tuple-element.16.grad, f32[2,768,768]{2,1,0:T(8,128)} %get-tuple-element.14.specimen_ref.extended, f32[2,256,256]{2,1,0:T(8,128)S(1)} %get-tuple-element.15.probe_ref.probe, f32[2,256,256]{2,1,0:T(8,128)S(1)} %get-tuple-element.17.probe_grad), custom_call_target="tpu_custom_call" | custom-call | tf_op jit(solution)/shard_map/fold/pallas_call | solution.py:850
  225.8 1.3 copy.17
  227.1 0.8 copy.18
  (1 shorter events, 0.0 us)
Async XLA Ops:
  2.1 1.6 copy-start
  3.7 1.4 copy-start.2
  5.1 1.0 copy-start.7
  6.1 1.0 copy-start.8
  7.1 33.4 %copy-start.1 = (f32[2,256,256]{2,1,0:T(8,128)S(1)}, f32[2,256,256]{2,1,0:T(8,128)}, u32[]{:S(2)}) copy-start(f32[2,256,256]{2,1,0:T(8,128)} %probe.1) | copy-start | bytes 1572868
  7.1 33.4 %copy-start.3 = (bf16[768,256]{1,0:T(8,128)(2,1)S(1)}, bf16[768,256]{1,0:T(8,128)(2,1)}, u32[]{:S(2)}) copy-start(bf16[768,256]{1,0:T(8,128)(2,1)} %constant.24.clone.right_back_ref) | copy-start | bytes 1179652
  7.1 33.4 %copy-start.4 = (bf16[256,768]{1,0:T(8,128)(2,1)S(1)}, bf16[256,768]{1,0:T(8,128)(2,1)}, u32[]{:S(2)}) copy-start(bf16[256,768]{1,0:T(8,128)(2,1)} %constant.23.clone.left_back_ref) | copy-start | bytes 1179652
  7.1 33.4 %copy-start.5 = (bf16[768,256]{1,0:T(8,128)(2,1)S(1)}, bf16[768,256]{1,0:T(8,128)(2,1)}, u32[]{:S(2)}) copy-start(bf16[768,256]{1,0:T(8,128)(2,1)} %constant.22.clone.right_ref) | copy-start | bytes 1179652
  7.1 33.4 %copy-start.6 = (bf16[256,768]{1,0:T(8,128)(2,1)S(1)}, bf16[256,768]{1,0:T(8,128)(2,1)}, u32[]{:S(2)}) copy-start(bf16[256,768]{1,0:T(8,128)(2,1)} %constant.21.clone.left_ref) | copy-start | bytes 1179652

commit v3 on v2

v3 whole, which is shorter than its diff:
```python
import functools

import jax
import jax.numpy as jnp
import ml_dtypes
import numpy as np
from jax import lax
from jax.experimental import pallas as pl
from jax.experimental.pallas import tpu as pltpu
from jax.sharding import PartitionSpec as P

POS_DEV = 3
ITERS = 2
OBJECT_STEP = 0.05
PROBE_GAIN = 0.5
MESH = pl.DeviceIdType.MESH
VMEM_LIMIT = 48 * 1024 * 1024
SUBLANES = 8
TOGETHER = 3


def real_table(window):
    half = window // 2
    k = np.arange(window)
    freq = np.where(k <= half, k, k - half)
    angles = 2.0 * np.pi * ((freq[:, None] * k[None, :]) % window) / window
    table = np.where((k <= half)[:, None], np.cos(angles), np.sin(angles))
    return table / np.sqrt(window)


def split_table(table):
    high = table.astype(ml_dtypes.bfloat16)
    low = (table - high.astype(np.float64)).astype(ml_dtypes.bfloat16)
    return high, low


def tables(window):
    high, low = split_table(real_table(window))
    return [jnp.asarray(t) for t in (high, low, high.T, low.T)]


def split(value):
    high = value.astype(jnp.bfloat16)
    low = (value - high.astype(jnp.float32)).astype(jnp.bfloat16)
    return high, low


def dot(left, right):
    return jnp.dot(left, right, preferred_element_type=jnp.float32)


def left_product(table, value):
    high, low = split(value)
    return dot(table[0][...], high) + dot(table[1][...], high) + dot(table[0][...], low)


def right_product(value, table):
    high, low = split(value)
    return dot(high, table[0][...]) + dot(high, table[1][...]) + dot(low, table[0][...])


def compute_kernel(
    count_ref, offsets_ref, specimen_ref, probe_ref, measured_ref,
    high_ref, low_ref, high_t_ref, low_t_ref,
    grad_ref, probe_grad_ref,
    windows, levels, window_sems, level_sems,
):
    table, table_t = (high_ref, low_ref), (high_t_ref, low_t_ref)
    window = probe_ref.shape[1]
    half = window // 2
    lanes = 128
    blocks = window // lanes
    lane = lax.broadcasted_iota(jnp.int32, (window + SUBLANES, lanes), 1)
    sublane = lax.broadcasted_iota(jnp.int32, (window // SUBLANES, SUBLANES, lanes), 1)
    sublane_ext = lax.broadcasted_iota(jnp.int32, (window // SUBLANES + 1, SUBLANES, lanes), 1)
    first_row = lax.broadcasted_iota(jnp.int32, (half, window), 0) == 0
    first_col = lax.broadcasted_iota(jnp.int32, (window, half), 1) == 0

    probe_real, probe_imag = probe_ref[0], probe_ref[1]

    def position(slot):
        row = offsets_ref[slot, 0]
        col = offsets_ref[slot, 1]
        row_block = pl.multiple_of((row // SUBLANES) * SUBLANES, SUBLANES)
        col_block = pl.multiple_of((col // lanes) * lanes, lanes)
        return row_block, col_block, row - row_block, col - col_block

    def place(where, part, j):
        return (
            part,
            pl.ds(where[0], window + SUBLANES),
            pl.ds(pl.multiple_of(where[1] + lanes * j, lanes), lanes),
        )

    def loads(slot):
        row_block, col_block, _, _ = position(slot)
        rows, cols = pl.ds(row_block, window + SUBLANES), pl.ds(col_block, window + lanes)
        return (
            pltpu.make_async_copy(specimen_ref.at[:, rows, cols], windows.at[slot], window_sems.at[slot]),
            pltpu.make_async_copy(measured_ref.at[slot], levels.at[slot], level_sems.at[slot]),
        )

    def cut(slot, where, part):
        row_rest, col_rest = where[2:]
        keep = lane < lanes - col_rest
        pieces = [
            pltpu.roll(
                windows[slot, part, :, lanes * j:lanes * (j + 1)], lax.rem(lanes - col_rest, lanes), 1)
            for j in range(blocks + 1)
        ]
        columns = []
        for j in range(blocks):
            taken = jnp.where(keep, pieces[j], pieces[j + 1])
            taken = taken.reshape(window // SUBLANES + 1, SUBLANES, lanes)
            taken = pltpu.roll(taken, lax.rem(SUBLANES - row_rest, SUBLANES), 1)
            upper = sublane < SUBLANES - row_rest
            columns.append(jnp.where(upper, taken[:-1], taken[1:]).reshape(window, lanes))
        return jnp.concatenate(columns, axis=1)

    def add_term(where, part, term):
        row_rest, col_rest = where[2:]
        before = lane < col_rest
        above = sublane_ext < row_rest
        turned = []
        for j in range(blocks):
            piece = term[:, lanes * j:lanes * (j + 1)]
            piece = piece.reshape(window // SUBLANES, SUBLANES, lanes)
            piece = pltpu.roll(piece, row_rest, 1)
            edge = jnp.zeros((1, SUBLANES, lanes), jnp.float32)
            piece = jnp.where(
                above,
                jnp.concatenate([edge, piece], axis=0),
                jnp.concatenate([piece, edge], axis=0),
            ).reshape(window + SUBLANES, lanes)
            turned.append(pltpu.roll(piece, col_rest, 1))
        for j in range(blocks + 1):
            if j == 0:
                add = jnp.where(before, 0.0, turned[0])
            elif j == blocks:
                add = jnp.where(before, turned[-1], 0.0)
            else:
                add = jnp.where(before, turned[j - 1], turned[j])
            grad_ref[place(where, part, j)] += add

    def exit_wave(patch):
        real, imag = patch
        psi_real = probe_real * real - probe_imag * imag
        psi_imag = probe_real * imag + probe_imag * real
        return jnp.concatenate([psi_real, psi_imag], axis=1)

    def unfold_rows(both):
        u_top, v_top = both[:half, :window], both[:half, window:]
        u_bot, v_bot = both[half:, :window], both[half:, window:]
        u_add = jnp.where(first_row, 0.0, u_bot)
        v_add = jnp.where(first_row, 0.0, v_bot)
        return jnp.concatenate([
            u_top + v_add, jnp.where(first_row, u_bot, u_top - v_bot),
            v_top - u_add, jnp.where(first_row, v_bot, v_top + u_bot)], axis=0)

    def unfold_cols(both):
        u_top, v_top = both[:window, :half], both[window:, :half]
        u_bot, v_bot = both[:window, half:], both[window:, half:]
        u_add = jnp.where(first_col, 0.0, u_bot)
        v_add = jnp.where(first_col, 0.0, v_bot)
        far_real = jnp.concatenate([u_top + v_add, jnp.where(first_col, u_bot, u_top - v_bot)], axis=1)
        far_imag = jnp.concatenate([v_top - u_add, jnp.where(first_col, v_bot, v_top + u_bot)], axis=1)
        return far_real, far_imag

    def fold_rows(g_real, g_imag):
        r_top, r_bot = g_real[:half], g_real[half:]
        i_top, i_bot = g_imag[:half], g_imag[half:]
        z_real = jnp.concatenate(
            [r_top + jnp.where(first_row, 0.0, r_bot), jnp.where(first_row, r_bot, i_bot - i_top)], axis=0)
        z_imag = jnp.concatenate(
            [i_top + jnp.where(first_row, 0.0, i_bot), jnp.where(first_row, i_bot, r_top - r_bot)], axis=0)
        return jnp.concatenate([z_real, z_imag], axis=1)

    def fold_cols(both):
        r_top, r_bot = both[:, :half], both[:, half:window]
        i_top, i_bot = both[:, window:window + half], both[:, window + half:]
        z_real = jnp.concatenate(
            [r_top + jnp.where(first_col, 0.0, r_bot), jnp.where(first_col, r_bot, i_bot - i_top)], axis=1)
        z_imag = jnp.concatenate(
            [i_top + jnp.where(first_col, 0.0, i_bot), jnp.where(first_col, i_bot, r_top - r_bot)], axis=1)
        return jnp.concatenate([z_real, z_imag], axis=0)

    def visit(step, carry):
        slots = [TOGETHER * step + i for i in range(TOGETHER)]
        where = [position(slot) for slot in slots]
        live = [(slot < count_ref[0]).astype(jnp.float32) for slot in slots]
        for slot in slots:
            for copy in loads(slot):
                copy.wait()
        patches = [(cut(slot, w, 0), cut(slot, w, 1)) for slot, w in zip(slots, where)]
        waves = [left_product(table, exit_wave(patch)) for patch in patches]
        waves = [right_product(unfold_rows(wave), table_t) for wave in waves]
        sources = []
        for wave, slot, on in zip(waves, slots, live):
            far_real, far_imag = unfold_cols(wave)
            factor = on * (far_real * far_real + far_imag * far_imag - levels[slot])
            sources.append(fold_rows(factor * far_real, factor * far_imag))
        waves = [left_product(table_t, source) for source in sources]
        waves = [right_product(fold_cols(wave), table) for wave in waves]
        for wave, patch, w in zip(waves, patches, where):
            chi_real, chi_imag = wave[:window], wave[window:]
            probe_grad_ref[0] += patch[0] * chi_real + patch[1] * chi_imag
            probe_grad_ref[1] += patch[0] * chi_imag - patch[1] * chi_real
            add_term(w, 0, probe_real * chi_real + probe_imag * chi_imag)
            add_term(w, 1, probe_real * chi_imag - probe_imag * chi_real)
        return carry

    steps = (count_ref[0] + TOGETHER - 1) // TOGETHER

    def fetch_slot(slot, carry):
        for copy in loads(slot):
            copy.start()
        return carry

    lax.fori_loop(0, steps * TOGETHER, fetch_slot, 0)
    grad_ref[...] = jnp.zeros_like(grad_ref)
    probe_grad_ref[...] = jnp.zeros_like(probe_grad_ref)
    lax.fori_loop(0, steps, visit, 0)


def slot_gradients(count, offsets, extended, illumination, measured, dft):
    smem = pl.BlockSpec(memory_space=pltpu.SMEM)
    vmem = pl.BlockSpec(memory_space=pltpu.VMEM)
    hbm = pl.BlockSpec(memory_space=pl.ANY)
    slots, window, _ = measured.shape
    return pl.pallas_call(
        compute_kernel,
        out_shape=(
            jax.ShapeDtypeStruct(extended.shape, jnp.float32),
            jax.ShapeDtypeStruct(illumination.shape, jnp.float32),
        ),
        in_specs=[smem, smem, hbm, vmem, hbm] + [vmem] * 4,
        out_specs=(vmem, vmem),
        scratch_shapes=[
            pltpu.VMEM((slots, 2, window + SUBLANES, window + 128), jnp.float32),
            pltpu.VMEM(measured.shape, jnp.float32),
            pltpu.SemaphoreType.DMA((slots,)),
            pltpu.SemaphoreType.DMA((slots,)),
        ],
        compiler_params=pltpu.CompilerParams(vmem_limit_bytes=VMEM_LIMIT),
        name="slot_gradients",
    )(count, offsets, extended, illumination, measured, *dft)


def place_of():
    return lax.axis_index("ty"), lax.axis_index("tx"), lax.axis_size("ty"), lax.axis_size("tx")


def send_to(source, target, sems, index, row, col):
    send_sem, recv_sem = sems
    return pltpu.make_async_remote_copy(
        src_ref=source,
        dst_ref=target,
        send_sem=send_sem.at[index],
        recv_sem=recv_sem.at[index],
        device_id=(row, col),
        device_id_type=MESH,
    )


def wait_bytes(ref, sem):
    pltpu.make_async_copy(ref, ref, sem).wait()


def greet(partners):
    barrier = pltpu.get_barrier_semaphore()
    for exists, row, col in partners:
        @pl.when(exists)
        def _():
            pl.semaphore_signal(barrier, inc=1, device_id=(row, col), device_id_type=MESH)
    pl.semaphore_wait(barrier, sum(jnp.int32(exists) for exists, _, _ in partners))


class Boundary:
    LINES = 4

    def __init__(self, relay, sems):
        self.relay = relay
        self.first_send, self.hop_recv, self.hop_send, self.last_recv = sems
        self.a, self.b, _, n = place_of()
        half = n // 2
        self.low, self.high = half - 1, half
        if n >= 16:
            inner = ((half, half + 3, 3, half - 1), (half, n - 4, half - 4, half - 1))
        else:
            inner = ((half, half + 2, 2, half - 1), (half, n - 3, half - 3, half - 1))
        self.paths = ((half, 0, half - 1), *inner, (half, n - 1, half - 1))
        self.at_low, self.at_high = self.b == self.low, self.b == self.high

    @staticmethod
    def scratch(window):
        return [
            pltpu.VMEM((2, 3, window // 2, window), jnp.float32),
            pltpu.SemaphoreType.DMA((2, 3, Boundary.LINES)),
            pltpu.SemaphoreType.DMA((2, 3)),
            pltpu.SemaphoreType.DMA((2, 3)),
            pltpu.SemaphoreType.DMA((2, 3, Boundary.LINES)),
        ]

    def partners(self, every):
        pairs = sorted({tuple(sorted(pair)) for path in self.paths for pair in zip(path, path[1:])})
        found = []
        for p, q in pairs:
            if p // 2 != q // 2 and (every or p % 2 != q % 2):
                found += [(self.b == p, self.a, q), (self.b == q, self.a, p)]
        return found

    def path(self, way, line):
        return self.paths[line] if way == 1 else self.paths[line][::-1]

    def origin(self, way):
        return self.low if way == 0 else self.high

    @staticmethod
    def quarter(ref, line):
        rows = ref.shape[1] // 2
        return ref.at[line // 2, pl.ds(line % 2 * rows, rows), :]

    def leg(self, way, index, line, k, source, target):
        path = self.path(way, line)
        last = k == len(path) - 2
        return pltpu.make_async_remote_copy(
            src_ref=self.quarter(source, line) if k == 0 else self.relay.at[way, index],
            dst_ref=self.quarter(target, line) if last else self.relay.at[way, index],
            send_sem=self.first_send.at[way, index, line] if k == 0 else self.hop_send.at[way, index],
            recv_sem=self.last_recv.at[way, index, line] if last else self.hop_recv.at[way, index],
            device_id=(self.a, path[k + 1]),
            device_id_type=MESH,
        )

    def start(self, way, index, source, target):
        for line in range(self.LINES):
            self.leg(way, index, line, 0, source, target).start()

    def relays(self, way):
        return [(line, k, node) for line in range(self.LINES)
                for k, node in enumerate(self.path(way, line)) if 0 < k < len(self.path(way, line)) - 1]

    def pass_on(self, way, index, source, target):
        for line, k, node in self.relays(way):
            @pl.when(self.b == node)
            def _():
                self.leg(way, index, line, k - 1, source, target).wait_recv()
                self.leg(way, index, line, k, source, target).start()

    def passed(self, way, index, source, target):
        for line, k, node in self.relays(way):
            @pl.when(self.b == node)
            def _():
                self.leg(way, index, line, k, source, target).wait_send()

    def wait_recv(self, way, index, source, target):
        for line in range(self.LINES):
            self.leg(way, index, line, len(self.path(way, line)) - 2, source, target).wait_recv()

    def wait_send(self, way, index, source, target):
        for line in range(self.LINES):
            self.leg(way, index, line, 0, source, target).wait_send()


class Sideways:
    def __init__(self, boundary, way, index, source, target, sems, slot):
        a, b, _, n_tx = place_of()
        self.boundary = boundary
        self.strip = (way, index, source, target)
        step = 1 if way == 0 else -1
        self.direct = send_to(source, target, sems, slot, a, b + step)
        left, right = b > 0, b < n_tx - 1
        self.has_target, self.has_source = (right, left) if way == 0 else (left, right)
        self.from_origin = b == boundary.origin(way)
        self.at_end = b == boundary.origin(1 - way)

    def start(self):
        self.start_relayed()
        self.start_direct()

    def start_relayed(self):
        pl.when(self.from_origin)(lambda: self.boundary.start(*self.strip))

    def start_direct(self):
        pl.when(self.has_target & ~self.from_origin)(self.direct.start)

    def pass_on(self):
        self.boundary.pass_on(*self.strip)

    def wait_recv(self):
        pl.when(self.at_end)(lambda: self.boundary.wait_recv(*self.strip))
        pl.when(self.has_source & ~self.at_end)(self.direct.wait_recv)

    def wait_send(self):
        pl.when(self.from_origin)(lambda: self.boundary.wait_send(*self.strip))
        pl.when(self.has_target & ~self.from_origin)(self.direct.wait_send)

    def passed(self):
        self.boundary.passed(*self.strip)


def fetch_kernel(
    specimen, patterns, extended, measured_out,
    measured, send, recv, local, *rest,
):
    a, b, n_ty, n_tx = place_of()
    window = measured.shape[1]
    tile = specimen.shape[1]
    half = window // 2
    up, down, left, right = a > 0, a < n_ty - 1, b > 0, b < n_tx - 1
    boundary = Boundary(rest[0], rest[1:])
    near = (True, a, b + 1 - 2 * lax.rem(b, 2))
    greet([(up, a - 1, b), (down, a + 1, b), near, far_neighbour(a, b, n_tx)] + boundary.partners(True))
    sems = (send, recv)
    first, second = pl.ds(0, window), pl.ds(window, tile - window)
    beyond, inside = pl.ds(tile, window), pl.ds(0, tile)

    def aside(index, source, rows):
        return Sideways(
            boundary, 1, index, source.at[:, rows, first], extended.at[:, rows, beyond], sems, 2 + index)

    up_a = send_to(specimen.at[:, first, first], extended.at[:, beyond, first], sems, 0, a - 1, b)
    up_b = send_to(specimen.at[:, first, second], extended.at[:, beyond, second], sems, 1, a - 1, b)
    aside_a = aside(0, specimen, first)
    aside_b = aside(1, specimen, second)
    corner = send_to(
        extended.at[:, beyond, first], extended.at[:, beyond, beyond], sems, 4, a, b - 1)
    corner_up = send_to(
        extended.at[:, first, beyond], extended.at[:, beyond, beyond], sems, 5, a - 1, b)
    corner_left = down & left & ~boundary.at_high
    keep = pltpu.make_async_copy(specimen, extended.at[:, inside, inside], local.at[0])
    load = pltpu.make_async_copy(patterns.at[0], measured, local.at[1])
    pl.when(up)(up_a.start)
    aside_a.start()
    aside_b.start()
    load.start()
    keep.start()
    aside_a.pass_on()

    @pl.when(up)
    def _():
        up_a.wait_send()
        up_b.start()

    aside_b.pass_on()

    pl.when(down)(up_a.wait_recv)
    pl.when(corner_left)(corner.start)

    @pl.when(boundary.at_low)
    def _():
        aside_a.wait_recv()
        pl.when(up)(corner_up.start)

    load.wait()
    row = lax.broadcasted_iota(jnp.int32, (window, window), 0)
    col = lax.broadcasted_iota(jnp.int32, (window, window), 1)

    def order(place, freq):
        picked = jnp.where(place <= half, place, window + half - place) == freq
        return picked.astype(jnp.float32).astype(jnp.bfloat16)

    reorder = jnp.concatenate([order(row, col)] * 3, axis=1)
    reorder_back = jnp.concatenate([order(col, row)] * 3, axis=0)

    def rearrange(slot, carry):
        def pieces(value):
            high, low = split(value)
            rest = (value - high.astype(jnp.float32) - low.astype(jnp.float32)).astype(jnp.bfloat16)
            return [high, low, rest]

        rows = jnp.dot(
            reorder, jnp.concatenate(pieces(measured[slot]), axis=0), preferred_element_type=jnp.float32)
        measured_out[slot] = jnp.dot(
            jnp.concatenate(pieces(rows), axis=1), reorder_back, preferred_element_type=jnp.float32)
        return carry

    lax.fori_loop(0, measured.shape[0], rearrange, 0)
    keep.wait()
    pl.when(~boundary.at_low)(aside_a.wait_recv)
    aside_b.wait_recv()
    pl.when(up)(up_b.wait_send)
    pl.when(down)(up_b.wait_recv)
    pl.when(corner_left)(corner.wait_send)
    pl.when(down & right & ~boundary.at_low)(corner.wait_recv)

    @pl.when(boundary.at_low)
    def _():
        pl.when(up)(corner_up.wait_send)
        pl.when(down)(corner_up.wait_recv)

    for strip in (aside_a, aside_b):
        strip.wait_send()
        strip.passed()


def fetch(specimen, patterns):
    window = patterns.shape[2]
    side = specimen.shape[1] + window
    vmem = pl.BlockSpec(memory_space=pltpu.VMEM)
    hbm = pl.BlockSpec(memory_space=pl.ANY)
    return pl.pallas_call(
        fetch_kernel,
        out_shape=(
            jax.ShapeDtypeStruct((2, side, side), jnp.float32),
            jax.ShapeDtypeStruct(patterns.shape[1:], jnp.float32),
        ),
        in_specs=[hbm, hbm],
        out_specs=(hbm, vmem),
        scratch_shapes=[
            pltpu.VMEM(patterns.shape[1:], jnp.float32),
            pltpu.SemaphoreType.DMA((6,)),
            pltpu.SemaphoreType.DMA((6,)),
            pltpu.SemaphoreType.DMA((2,)),
        ] + Boundary.scratch(window),
        compiler_params=pltpu.CompilerParams(
            collective_id=0, has_side_effects=True, vmem_limit_bytes=VMEM_LIMIT),
        name="fetch",
    )(specimen, patterns)


class ProbeSum:
    STAGES = 7

    def __init__(self, terms, buffers, send, recv):
        self.terms = terms
        self.mate, self.mine, self.y_in, self.y_sum, self.z_in, self.x_in, self.z_out, self.full, self.other = buffers
        self.send, self.recv = send, recv
        self.a, self.b, n_ty, n_tx = place_of()
        self.n_x, self.n_y, self.n_z = self.sizes(n_ty, n_tx)
        self.n_low = self.n_z // 2
        self.devices = n_ty * n_tx
        self.core = lax.rem(self.b, 2)
        self.y = lax.rem(self.b // 2, self.n_y)
        self.x = lax.rem(self.a, self.n_x)
        self.z = self.b // (2 * self.n_y) * self.n_low + self.a // self.n_x
        self.mate_col = self.b + 1 - 2 * self.core
        self.y_rows = self.full.shape[0] // self.n_y
        self.z_rows = self.y_rows // self.n_z

    @staticmethod
    def sizes(n_ty, n_tx):
        n_x = 4 if n_ty == 16 else 2
        return n_x, n_tx // 4, 2 * (n_ty // n_x)

    @staticmethod
    def scratch(window, n_ty, n_tx):
        n_x, n_y, n_z = ProbeSum.sizes(n_ty, n_tx)
        y_rows = window // n_y
        z_rows = y_rows // n_z
        shapes = [
            (window, window), (window, window), (n_y - 1, y_rows, window), (y_rows, window),
            (n_z - 1, z_rows, window), (n_x, z_rows, window), (y_rows, window),
            (window, window), (window, window),
        ]
        return [pltpu.VMEM(shape, jnp.float32) for shape in shapes] + [
            pltpu.SemaphoreType.DMA((ProbeSum.STAGES,)),
            pltpu.SemaphoreType.DMA((ProbeSum.STAGES,)),
        ]

    def at_y(self, y):
        return self.a, (self.b // (2 * self.n_y)) * 2 * self.n_y + 2 * y + self.core

    def at_z(self, z):
        return lax.rem(z, self.n_low) * self.n_x + self.x, (z // self.n_low) * 2 * self.n_y + 2 * self.y + self.core

    def at_x(self, x):
        return self.a - self.x + x, self.b

    def partners(self):
        found = [(True, self.a, self.mate_col)]
        found += [(True, *self.at_y(lax.rem(self.y + d, self.n_y))) for d in range(1, self.n_y)]
        found += [(True, *self.at_z(lax.rem(self.z + d, self.n_z))) for d in range(1, self.n_z)]
        found += [(True, *self.at_x(lax.rem(self.x + d, self.n_x))) for d in range(1, self.n_x)]
        n_ty = self.n_low * self.n_x
        wraps_down = (self.x == self.n_x - 1) & (self.a < n_ty - 1)
        wraps_up = (self.x == 0) & (self.a > 0)
        found.append((wraps_down | wraps_up, jnp.where(wraps_up, self.a - 1, self.a + 1), self.b))
        return found

    def to(self, source, target, stage, row, col):
        return send_to(source, target, (self.send, self.recv), stage, row, col)

    @staticmethod
    def rows(ref, index, count):
        return ref.at[pl.ds(pl.multiple_of(index * count, SUBLANES), count), :]

    def each(self, count, go):
        def step(d, carry):
            go(d)
            return carry

        lax.fori_loop(1, count, step, 0)

    def start(self):
        self.to(self.terms.at[1 - self.core], self.mate, 0, self.a, self.mate_col).start()

    def scatter_y(self):
        self.to(self.terms.at[1 - self.core], self.mate, 0, self.a, self.mate_col).wait()
        self.mine[...] = self.terms[self.core] + self.mate[...]

        def go(d):
            y = lax.rem(self.y + d, self.n_y)
            self.to(self.rows(self.mine, y, self.y_rows), self.y_in.at[d - 1], 1, *self.at_y(y)).start()

        self.each(self.n_y, go)

    def scatter_z(self):
        wait_bytes(self.y_in, self.recv.at[1])
        total = self.rows(self.mine, self.y, self.y_rows)[...]
        for d in range(self.n_y - 1):
            total = total + self.y_in[d]
        self.y_sum[...] = total

        def go(d):
            z = lax.rem(self.z + d, self.n_z)
            self.to(self.rows(self.y_sum, z, self.z_rows), self.z_in.at[d - 1], 2, *self.at_z(z)).start()

        self.each(self.n_z, go)

    def across_x(self):
        wait_bytes(self.z_in, self.recv.at[2])
        total = self.rows(self.y_sum, self.z, self.z_rows)[...]
        for d in range(self.n_z - 1):
            total = total + self.z_in[d]
        self.x_in[self.x] = total

        def go(d):
            x = lax.rem(self.x + d, self.n_x)
            self.to(self.x_in.at[self.x], self.x_in.at[self.x], 3, *self.at_x(x)).start()

        self.each(self.n_x, go)

    def gather_z(self):
        wait_bytes(self.x_in.at[pl.ds(0, self.n_x - 1)], self.recv.at[3])
        total = self.x_in[0]
        for i in range(1, self.n_x):
            total = total + self.x_in[i]
        own = self.rows(self.z_out, self.z, self.z_rows)
        own[...] = total

        def go(d):
            z = lax.rem(self.z + d, self.n_z)
            self.to(own, own, 4, *self.at_z(z)).start()

        self.each(self.n_z, go)

    def gather_y(self):
        wait_bytes(self.z_out.at[pl.ds(0, (self.n_z - 1) * self.z_rows)], self.recv.at[4])
        own = self.rows(self.full, self.y, self.y_rows)
        own[...] = self.z_out[...]

        def go(d):
            y = lax.rem(self.y + d, self.n_y)
            self.to(self.z_out, own, 5, *self.at_y(y)).start()

        self.each(self.n_y, go)

    def share(self):
        wait_bytes(self.full.at[pl.ds(0, (self.n_y - 1) * self.y_rows)], self.recv.at[5])
        self.to(self.full, self.other, 6, self.a, self.mate_col).start()

    def finish(self, probe, probe_out):
        step = PROBE_GAIN / (POS_DEV * self.devices)
        probe_out[self.core] = probe[self.core] - step * self.full[...]
        self.to(self.full, self.other, 6, self.a, self.mate_col).wait()
        probe_out[1 - self.core] = probe[1 - self.core] - step * self.other[...]
        wait_bytes(self.y_in, self.send.at[1])
        wait_bytes(self.z_in, self.send.at[2])
        wait_bytes(self.x_in.at[pl.ds(0, self.n_x - 1)], self.send.at[3])
        wait_bytes(self.z_out.at[pl.ds(0, (self.n_z - 1) * self.z_rows)], self.send.at[4])
        wait_bytes(self.full.at[pl.ds(0, (self.n_y - 1) * self.y_rows)], self.send.at[5])


def far_neighbour(a, b, n_tx):
    core = lax.rem(b, 2)
    col = b - 1 + 2 * core
    return ((col >= 0) & (col < n_tx) & (b != n_tx // 2 - 1) & (b != n_tx // 2), a, col)


def exchange_kernel(
    grad, extended, probe, probe_grad, extended_out, probe_out,
    gv, ev, from_left, from_right, from_up, from_down, send, recv, local,
    *rest,
):
    a, b, n_ty, n_tx = place_of()
    window = probe.shape[1]
    side = gv.shape[1]
    tile = side - window
    core = lax.rem(b, 2)
    has_up, has_down, has_left, has_right = a > 0, a < n_ty - 1, b > 0, b < n_tx - 1
    odd = core == 1
    total = ProbeSum(probe_grad, rest[:9], *rest[9:11])
    boundary = Boundary(rest[11], rest[12:])
    greet(total.partners() + [far_neighbour(a, b, n_tx)] + boundary.partners(False))
    sems = (send, recv)
    start, middle, end = pl.ds(0, window), pl.ds(window, tile - window), pl.ds(tile, window)

    def across(rows, index):
        return (
            Sideways(boundary, 0, index, grad.at[:, rows, end], from_left.at[:, rows, :], sems, 2 * index),
            Sideways(boundary, 1, index, grad.at[:, rows, start], from_right.at[:, rows, :], sems, 2 * index + 1),
        )

    def along(source, cols, index):
        return (
            send_to(source.at[:, end, cols], from_up.at[:, :, cols], sems, index, a + 1, b),
            send_to(source.at[:, start, cols], from_down.at[:, :, cols], sems, index + 1, a - 1, b),
        )

    right_top, left_top = across(start, 0)
    right_end, left_end = across(end, 1)
    right_mid, left_mid = across(middle, 2)
    down_1, up_1 = along(grad, middle, 6)
    down_0, up_0 = along(gv, start, 8)
    down_2, up_2 = along(gv, end, 10)
    keep_top = send_to(ev.at[:, start, start], extended_out.at[:, start, end], sems, 12, a, b - 1)
    keep_end = send_to(ev.at[:, end, start], extended_out.at[:, end, end], sems, 13, a, b - 1)

    load_grad = pltpu.make_async_copy(grad, gv, local.at[0])
    load_extended = pltpu.make_async_copy(extended, ev, local.at[1])

    outer = (right_top, right_end, left_top, left_end)
    total.start()
    right_top.start()
    left_top.start()
    pl.when(has_down)(down_1.start)
    pl.when(has_up)(up_1.start)
    load_grad.start()
    load_extended.start()
    total.scatter_y()
    right_end.start()
    left_end.start()
    right_mid.start_relayed()
    left_mid.start_relayed()
    right_top.pass_on()
    left_top.pass_on()
    total.scatter_z()
    right_end.pass_on()
    left_end.pass_on()
    total.across_x()
    late = boundary.at_low | boundary.at_high

    @pl.when(late)
    def _():
        total.gather_z()
        total.gather_y()

    load_grad.wait()
    right_top.wait_recv()
    right_end.wait_recv()

    @pl.when(has_left)
    def _():
        gv[:, start, start] += from_left[:, start, :]
        gv[:, end, start] += from_left[:, end, :]

    pl.when(has_down)(down_0.start)
    pl.when(has_up)(up_0.start)
    left_top.wait_recv()
    left_end.wait_recv()

    @pl.when(has_right)
    def _():
        gv[:, start, end] += from_right[:, start, :]
        gv[:, end, end] += from_right[:, end, :]

    pl.when(has_down & odd)(down_2.start)
    pl.when(has_up & odd)(up_2.start)

    @pl.when(~late)
    def _():
        total.gather_z()
        total.gather_y()

    for strip in outer:
        strip.wait_send()
    right_mid.start_direct()
    left_mid.start_direct()
    right_mid.pass_on()
    left_mid.pass_on()
    load_extended.wait()
    right_mid.wait_recv()
    left_mid.wait_recv()

    @pl.when(has_left)
    def _():
        gv[:, middle, start] += from_left[:, middle, :]

    @pl.when(has_right)
    def _():
        gv[:, middle, end] += from_right[:, middle, :]

    ev[:, middle, :] -= OBJECT_STEP * gv[:, middle, :]
    store_mid = pltpu.make_async_copy(ev.at[:, middle, :], extended_out.at[:, middle, :], local.at[0])
    store_mid.start()
    total.share()

    def update(rows, cols, received, exists):
        @pl.when(exists)
        def _():
            ev[:, rows, cols] -= OBJECT_STEP * (gv[:, rows, cols] + received[:, :, cols])

        @pl.when(jnp.logical_not(exists))
        def _():
            ev[:, rows, cols] -= OBJECT_STEP * gv[:, rows, cols]

    pl.when(has_up)(down_0.wait_recv)
    pl.when(has_down)(up_0.wait_recv)
    update(start, start, from_up, has_up)
    update(end, start, from_down, has_down)

    @pl.when(odd)
    def _():
        keep_top.start()
        keep_end.start()

    pl.when(has_up)(down_1.wait_recv)
    pl.when(has_down)(up_1.wait_recv)
    update(start, middle, from_up, has_up)
    update(end, middle, from_down, has_down)
    inner = pl.ds(0, tile)
    store_top = pltpu.make_async_copy(ev.at[:, start, inner], extended_out.at[:, start, inner], local.at[1])
    store_end = pltpu.make_async_copy(ev.at[:, end, inner], extended_out.at[:, end, inner], local.at[2])
    store_top.start()
    store_end.start()

    @pl.when(odd)
    def _():
        pl.when(has_up)(down_2.wait_recv)
        pl.when(has_down)(up_2.wait_recv)
        update(start, end, from_up, has_up)
        update(end, end, from_down, has_down)
        rim_top = pltpu.make_async_copy(ev.at[:, start, end], extended_out.at[:, start, end], local.at[3])
        rim_end = pltpu.make_async_copy(ev.at[:, end, end], extended_out.at[:, end, end], local.at[4])
        rim_top.start()
        rim_end.start()
        rim_top.wait()
        rim_end.wait()
        keep_top.wait_send()
        keep_end.wait_send()

    total.finish(probe, probe_out)
    right_mid.wait_send()
    left_mid.wait_send()
    for strip in outer + (right_mid, left_mid):
        strip.passed()

    @pl.when(has_down)
    def _():
        down_0.wait_send()
        down_1.wait_send()
        pl.when(odd)(down_2.wait_send)

    @pl.when(has_up)
    def _():
        up_0.wait_send()
        up_1.wait_send()
        pl.when(odd)(up_2.wait_send)

    store_mid.wait()
    store_top.wait()
    store_end.wait()

    @pl.when(jnp.logical_not(odd))
    def _():
        keep_top.wait_recv()
        keep_end.wait_recv()


def exchange(grad, extended, illumination, probe_grad):
    window = illumination.shape[1]
    side = grad.shape[1]
    vmem = pl.BlockSpec(memory_space=pltpu.VMEM)
    hbm = pl.BlockSpec(memory_space=pl.ANY)
    return pl.pallas_call(
        exchange_kernel,
        out_shape=(
            jax.ShapeDtypeStruct(extended.shape, jnp.float32),
            jax.ShapeDtypeStruct(illumination.shape, jnp.float32),
        ),
        in_specs=[hbm, hbm, vmem, vmem],
        out_specs=(hbm, vmem),
        scratch_shapes=[
            pltpu.VMEM((2, side, side), jnp.float32),
            pltpu.VMEM((2, side, side), jnp.float32),
            pltpu.VMEM((2, side, window), jnp.float32),
            pltpu.VMEM((2, side, window), jnp.float32),
            pltpu.VMEM((2, window, side), jnp.float32),
            pltpu.VMEM((2, window, side), jnp.float32),
            pltpu.SemaphoreType.DMA((14,)),
            pltpu.SemaphoreType.DMA((14,)),
            pltpu.SemaphoreType.DMA((5,)),
        ] + ProbeSum.scratch(window, lax.axis_size("ty"), lax.axis_size("tx")) + Boundary.scratch(window),
        compiler_params=pltpu.CompilerParams(
            collective_id=1, has_side_effects=True, vmem_limit_bytes=VMEM_LIMIT),
        name="exchange",
    )(grad, extended, illumination, probe_grad)


def fold_kernel(
    grad, extended, probe, probe_grad, specimen_out, probe_out,
    gv, ev, corner, from_left, from_up, send, recv, local,
    *rest,
):
    a, b, n_ty, n_tx = place_of()
    window = probe.shape[1]
    side = gv.shape[1]
    tile = side - window
    has_up, has_down, has_left, has_right = a > 0, a < n_ty - 1, b > 0, b < n_tx - 1
    total = ProbeSum(probe_grad, rest[:9], *rest[9:11])
    boundary = Boundary(rest[11], rest[12:])
    greet(total.partners() + [far_neighbour(a, b, n_tx)] + boundary.partners(False))
    sems = (send, recv)
    start, middle, end = pl.ds(0, window), pl.ds(window, tile - window), pl.ds(tile, window)
    inner = pl.ds(0, tile)

    def across(rows, index):
        return Sideways(boundary, 0, index, grad.at[:, rows, end], from_left.at[:, rows, :], sems, index)

    right_end = across(end, 0)
    right_top = across(start, 1)
    right_mid = across(middle, 2)
    down_1 = send_to(grad.at[:, end, middle], from_up.at[:, :, middle], sems, 3, a + 1, b)
    down_0 = send_to(corner, from_up.at[:, :, start], sems, 4, a + 1, b)
    load_grad = pltpu.make_async_copy(grad.at[:, :, inner], gv, local.at[0])
    load_extended = pltpu.make_async_copy(extended.at[:, inner, inner], ev, local.at[1])
    total.start()
    right_end.start()
    right_top.start_relayed()
    right_mid.start_relayed()
    pl.when(has_down)(down_1.start)
    load_grad.start()
    load_extended.start()
    total.scatter_y()
    right_top.start_direct()
    right_end.pass_on()
    total.scatter_z()
    right_top.pass_on()
    load_grad.wait()

    @pl.when(boundary.at_high)
    def _():
        total.across_x()
        total.gather_z()
        total.gather_y()

    right_end.wait_recv()

    @pl.when(has_left)
    def _():
        corner[...] = gv[:, end, start] + from_left[:, end, :]

    @pl.when(jnp.logical_not(has_left))
    def _():
        corner[...] = gv[:, end, start]

    @pl.when(~boundary.at_high)
    def _():
        total.across_x()

    pl.when(has_down)(down_0.start)

    @pl.when(~boundary.at_high)
    def _():
        total.gather_z()
        total.gather_y()

    right_end.wait_send()
    right_mid.start_direct()
    right_mid.pass_on()
    load_extended.wait()
    ev[...] -= OBJECT_STEP * gv[:, inner, :]
    total.share()
    right_top.wait_recv()
    right_mid.wait_recv()

    @pl.when(has_left)
    def _():
        ev[:, :, start] -= OBJECT_STEP * from_left[:, inner, :]

    @pl.when(has_up)
    def _():
        down_1.wait_recv()
        down_0.wait_recv()
        ev[:, start, :] -= OBJECT_STEP * from_up[...]

    specimen_out[...] = ev[...]
    total.finish(probe, probe_out)
    right_top.wait_send()
    right_mid.wait_send()
    for strip in (right_end, right_top, right_mid):
        strip.passed()

    @pl.when(has_down)
    def _():
        down_1.wait_send()
        down_0.wait_send()


def fold(grad, extended, illumination, probe_grad):
    window = illumination.shape[1]
    side = grad.shape[1]
    tile = side - window
    vmem = pl.BlockSpec(memory_space=pltpu.VMEM)
    hbm = pl.BlockSpec(memory_space=pl.ANY)
    return pl.pallas_call(
        fold_kernel,
        out_shape=(
            jax.ShapeDtypeStruct((2, tile, tile), jnp.float32),
            jax.ShapeDtypeStruct(illumination.shape, jnp.float32),
        ),
        in_specs=[hbm, hbm, vmem, vmem],
        out_specs=(vmem, vmem),
        scratch_shapes=[
            pltpu.VMEM((2, side, tile), jnp.float32),
            pltpu.VMEM((2, tile, tile), jnp.float32),
            pltpu.VMEM((2, window, window), jnp.float32),
            pltpu.VMEM((2, side, window), jnp.float32),
            pltpu.VMEM((2, window, tile), jnp.float32),
            pltpu.SemaphoreType.DMA((5,)),
            pltpu.SemaphoreType.DMA((5,)),
            pltpu.SemaphoreType.DMA((2,)),
        ] + ProbeSum.scratch(window, lax.axis_size("ty"), lax.axis_size("tx")) + Boundary.scratch(window),
        compiler_params=pltpu.CompilerParams(
            collective_id=2, has_side_effects=True, vmem_limit_bytes=VMEM_LIMIT),
        name="fold",
    )(grad, extended, illumination, probe_grad)


def body(specimen, illumination, patterns, scan_offsets, counts):
    window = illumination.shape[1]
    tile = specimen.shape[1]
    row_anchor = lax.axis_index("ty") * tile
    col_anchor = lax.axis_index("tx") * tile
    offsets = scan_offsets[0] - jnp.stack([row_anchor, col_anchor])[None, :].astype(jnp.int32)
    count = counts.reshape(1)
    dft = tables(window)
    extended, measured = fetch(specimen, patterns)
    for iteration in range(ITERS):
        grad, probe_grad = slot_gradients(count, offsets, extended, illumination, measured, dft)
        if iteration < ITERS - 1:
            extended, illumination = exchange(grad, extended, illumination, probe_grad)
        else:
            specimen, illumination = fold(grad, extended, illumination, probe_grad)
    return (specimen, illumination)


def solution(mesh):
    placed = (
        P(None, "ty", "tx"),
        P(),
        P("ty", "tx", None, None),
        P("ty", "tx", None),
        P("ty", "tx"),
    )
    return jax.shard_map(
        body, mesh=mesh, in_specs=placed, out_specs=(P(None, "ty", "tx"), P()), check_vma=False
    )
```

time: 228 us -> 195 us (0.86)
  Pallas kernels: 219 us -> 186 us
    pallas_call x1, Pallas kernels: 74.8 us -> 60.9 us  [fold(): pl.pallas_call(fold_kernel, out_shape=(jax.ShapeDtypeStruct((2, tile, til...]
    pallas_call x1, Pallas kernels: 86 us -> 77.1 us  [exchange(): pl.pallas_call(exchange_kernel, out_shape=(jax.ShapeDtypeStruct(extended....]
    pallas_call x2, Pallas kernels: 24.4 us -> 17.3 us  [slot_gradients(): pl.pallas_call(compute_kernel, out_shape=(jax.ShapeDtypeStruct(extended.s...]
    pallas_call x1, Pallas kernels: 33.3 us -> 30.8 us  [fetch(): pl.pallas_call(fetch_kernel, out_shape=(jax.ShapeDtypeStruct((2, side, si...]
    unnamed x20 -> x16, local copies, waits for them, and re-layouts: 7.12 us -> 5.13 us
where the time goes in v3:
time: 195 us; the launch traced here: 193 us
  Pallas kernels  186 us (95%)
  local copies, waits for them, and re-layouts  5.9 us (3%)
    pallas_call x1, Pallas kernels, exchange(): pl.pallas_call(exchange_kernel, out_shape=(jax.ShapeDtypeStruct(extended....  77.1 us
    pallas_call x1, Pallas kernels, fold(): pl.pallas_call(fold_kernel, out_shape=(jax.ShapeDtypeStruct((2, tile, til...  60.9 us
    pallas_call x1, Pallas kernels, fetch(): pl.pallas_call(fetch_kernel, out_shape=(jax.ShapeDtypeStruct((2, side, si...  30.8 us
    pallas_call x2, Pallas kernels, slot_gradients(): pl.pallas_call(compute_kernel, out_shape=(jax.ShapeDtypeStruct(extended.s...  17.3 us
    unnamed x16, local copies, waits for them, and re-layouts  5.13 us

profile of v3, /device:TPU:198, one launch (start us, length us, event | category | flops | bytes accessed | tf_op | source)
XLA Modules:
  0.0 193.5 jit_solution(4201651084184379417)
XLA Ops:
  0.6 0.0 copy-start
  1.3 0.1 pad_add_fusion
  1.4 0.8 copy.11
  2.2 0.0 copy-start.1
  2.2 1.6 copy-done.1
  3.8 0.0 copy-start.2
  3.8 1.4 copy-done.2
  5.2 0.0 copy-start.3
  5.2 0.0 copy-start.4
  5.2 0.0 copy-start.5
  5.2 0.0 copy-start.6
  5.2 30.8 %fetch.1 = (f32[2,768,768]{2,1,0:T(8,128)}, f32[6,256,256]{2,1,0:T(8,128)S(1)}) custom-call(f32[2,512,512]{2,1,0:T(8,128)S(1)} %copy-done.1, f32[1,6,256,256]{3,2,1,0:T(8,128)S(1)} %copy-done.2), custom_call_target="tpu_custom_call" | custom-call | tf_op jit(solution)/shard_map/fetch/pallas_call | solution.py:502
  36.0 0.0 copy-done
  36.0 0.0 copy-done.3
  36.0 0.0 copy-done.4
  36.0 0.0 copy-done.5
  36.0 0.0 copy-done.6
  36.0 8.7 %slot_gradients.2 = (f32[2,768,768]{2,1,0:T(8,128)}, f32[2,256,256]{2,1,0:T(8,128)S(1)}) custom-call(s32[1]{0:T(128)} %bitcast.4.count_ref, s32[6,2]{1,0:T(8,128)S(1)} %broadcast_subtract_fusion.offsets_ref, f32[2,768,768]{2,1,0:T(8,128)} %get-tuple-element.10.specimen_ref.extended, f32[2,256,256]{2,1,0:T(8,128)S(1)} %copy-done, ...), custom_call_target="tpu_custom_call" | custom-call | tf_op jit(solution)/shard_map/slot_gradients/pallas_call | solution.py:230
  44.7 77.1 %exchange.1 = (f32[2,768,768]{2,1,0:T(8,128)}, f32[2,256,256]{2,1,0:T(8,128)S(1)}) custom-call(f32[2,768,768]{2,1,0:T(8,128)} %get-tuple-element.12.grad, f32[2,768,768]{2,1,0:T(8,128)} %get-tuple-element.10.specimen_ref.extended, f32[2,256,256]{2,1,0:T(8,128)S(1)} %copy-done, f32[2,256,256]{2,1,0:T(8,128)S(1)} %get-tuple-element.13.probe_grad), custom_call_target="tpu_custom_call" | custom-call | tf_op jit(solution)/shard_map/exchange/pallas_call | solution.py:876
  121.8 8.6 %slot_gradients.3 = (f32[2,768,768]{2,1,0:T(8,128)}, f32[2,256,256]{2,1,0:T(8,128)S(1)}) custom-call(s32[1]{0:T(128)} %bitcast.5.count_ref, s32[6,2]{1,0:T(8,128)S(1)} %broadcast_subtract_fusion.offsets_ref, f32[2,768,768]{2,1,0:T(8,128)} %get-tuple-element.14.specimen_ref.extended, f32[2,256,256]{2,1,0:T(8,128)S(1)} %get-tuple-element.15.probe_ref.probe, ...), custom_call_target="tpu_custom_call" | custom-call | tf_op jit(solution)/shard_map/slot_gradients/pallas_call | solution.py:230
  130.4 60.9 %fold.1 = (f32[2,512,512]{2,1,0:T(8,128)S(1)}, f32[2,256,256]{2,1,0:T(8,128)S(1)}) custom-call(f32[2,768,768]{2,1,0:T(8,128)} %get-tuple-element.16.grad, f32[2,768,768]{2,1,0:T(8,128)} %get-tuple-element.14.specimen_ref.extended, f32[2,256,256]{2,1,0:T(8,128)S(1)} %get-tuple-element.15.probe_ref.probe, f32[2,256,256]{2,1,0:T(8,128)S(1)} %get-tuple-element.17.probe_grad), custom_call_target="tpu_custom_call" | custom-call | tf_op jit(solution)/shard_map/fold/pallas_call | solution.py:1007
  191.4 1.3 copy.15
  192.7 0.8 copy.16
  (1 shorter events, 0.0 us)
Async XLA Ops:
  0.6 35.4 %copy-start = (f32[2,256,256]{2,1,0:T(8,128)S(1)}, f32[2,256,256]{2,1,0:T(8,128)}, u32[]{:S(2)}) copy-start(f32[2,256,256]{2,1,0:T(8,128)} %probe.1) | copy-start | bytes 1572868
  2.2 1.6 copy-start.1
  3.8 1.4 copy-start.2
  5.2 30.8 %copy-start.3 = (bf16[256,256]{1,0:T(8,128)(2,1)S(1)}, bf16[256,256]{1,0:T(8,128)(2,1)}, u32[]{:S(2)}) copy-start(bf16[256,256]{1,0:T(8,128)(2,1)} %constant.20.clone.low_t_ref) | copy-start | bytes 393220
  5.2 30.8 %copy-start.4 = (bf16[256,256]{1,0:T(8,128)(2,1)S(1)}, bf16[256,256]{1,0:T(8,128)(2,1)}, u32[]{:S(2)}) copy-start(bf16[256,256]{1,0:T(8,128)(2,1)} %constant.19.clone.high_t_ref) | copy-start | bytes 393220
  5.2 30.8 %copy-start.5 = (bf16[256,256]{1,0:T(8,128)(2,1)S(1)}, bf16[256,256]{1,0:T(8,128)(2,1)}, u32[]{:S(2)}) copy-start(bf16[256,256]{1,0:T(8,128)(2,1)} %constant.18.clone.low_ref) | copy-start | bytes 393220
  5.2 30.8 %copy-start.6 = (bf16[256,256]{1,0:T(8,128)(2,1)S(1)}, bf16[256,256]{1,0:T(8,128)(2,1)}, u32[]{:S(2)}) copy-start(bf16[256,256]{1,0:T(8,128)(2,1)} %constant.17.clone.high_ref) | copy-start | bytes 393220

commit v4 on v3

--- a/solution.py
+++ b/solution.py
@@ -14,7 +14,7 @@
 OBJECT_STEP = 0.05
 PROBE_GAIN = 0.5
 MESH = pl.DeviceIdType.MESH
-VMEM_LIMIT = 48 * 1024 * 1024
+VMEM_LIMIT = 36 * 1024 * 1024
 SUBLANES = 8
 TOGETHER = 3
 
@@ -282,6 +282,7 @@
         self.relay = relay
         self.first_send, self.hop_recv, self.hop_send, self.last_recv = sems
         self.a, self.b, _, n = place_of()
+        self.n = n
         half = n // 2
         self.low, self.high = half - 1, half
         if n >= 16:
@@ -307,6 +308,16 @@
         for p, q in pairs:
             if p // 2 != q // 2 and (every or p % 2 != q % 2):
                 found += [(self.b == p, self.a, q), (self.b == q, self.a, p)]
+        return found
+
+    def before_z(self, way):
+        n_x, n_y, _ = ProbeSum.sizes(lax.axis_size("ty"), self.n)
+        high = 2 * n_y
+        nodes = sorted({p for line in range(self.LINES)
+                        for p, q in zip(self.path(way, line), self.path(way, line)[1:]) if (p >= high) != (q >= high)})
+        found = self.b == nodes[0]
+        for node in nodes[1:]:
+            found = found | (self.b == node)
         return found
 
     def path(self, way, line):
@@ -401,7 +412,7 @@
 
 def fetch_kernel(
     specimen, patterns, extended, measured_out,
-    measured, send, recv, local, *rest,
+    measured, staged, send, recv, local, *rest,
 ):
     a, b, n_ty, n_tx = place_of()
     window = measured.shape[1]
@@ -428,22 +439,32 @@
     corner_up = send_to(
         extended.at[:, first, beyond], extended.at[:, beyond, beyond], sems, 5, a - 1, b)
     corner_left = down & left & ~boundary.at_high
-    keep = pltpu.make_async_copy(specimen, extended.at[:, inside, inside], local.at[0])
+    stage = pltpu.make_async_copy(specimen, staged, local.at[0])
+    keep = pltpu.make_async_copy(staged, extended.at[:, inside, inside], local.at[2])
     load = pltpu.make_async_copy(patterns.at[0], measured, local.at[1])
-    pl.when(up)(up_a.start)
+    hold = (lax.rem(a, ProbeSum.sizes(n_ty, n_tx)[0]) == 0) & up & boundary.before_z(1)
+    pl.when(up & ~hold)(up_a.start)
     aside_a.start()
     aside_b.start()
     load.start()
+    stage.start()
+    stage.wait()
     keep.start()
-    aside_a.pass_on()
+
+    @pl.when(hold)
+    def _():
+        aside_a.pass_on()
+        aside_b.pass_on()
+        up_a.start()
+
+    pl.when(~hold)(aside_a.pass_on)
 
     @pl.when(up)
     def _():
         up_a.wait_send()
         up_b.start()
 
-    aside_b.pass_on()
-
+    pl.when(~hold)(aside_b.pass_on)
     pl.when(down)(up_a.wait_recv)
     pl.when(corner_left)(corner.start)
 
@@ -509,12 +530,13 @@
         out_specs=(hbm, vmem),
         scratch_shapes=[
             pltpu.VMEM(patterns.shape[1:], jnp.float32),
+            pltpu.VMEM(specimen.shape, jnp.float32),
             pltpu.SemaphoreType.DMA((6,)),
             pltpu.SemaphoreType.DMA((6,)),
-            pltpu.SemaphoreType.DMA((2,)),
+            pltpu.SemaphoreType.DMA((3,)),
         ] + Boundary.scratch(window),
         compiler_params=pltpu.CompilerParams(
-            collective_id=0, has_side_effects=True, vmem_limit_bytes=VMEM_LIMIT),
+            collective_id=0, has_side_effects=True, vmem_limit_bytes=VMEM_LIMIT + 26 * 1024 * 1024),
         name="fetch",
     )(specimen, patterns)
 

time: 195 us -> 187 us (0.959)
  Pallas kernels: 186 us -> 176 us
    pallas_call x2, Pallas kernels: 17.3 us -> 11.2 us  [slot_gradients(): pl.pallas_call(compute_kernel, out_shape=(jax.ShapeDtypeStruct(extended.s...]
    pallas_call x1, Pallas kernels: 77.1 us -> 73.8 us  [exchange(): pl.pallas_call(exchange_kernel, out_shape=(jax.ShapeDtypeStruct(extended....]
    unnamed x16 -> x18, local copies, waits for them, and re-layouts: 5.13 us -> 5.89 us
where the time goes in v4:
time: 187 us; the launch traced here: 185 us
  Pallas kernels  176 us (94%)
  local copies, waits for them, and re-layouts  6.65 us (4%)
    pallas_call x1, Pallas kernels, exchange(): pl.pallas_call(exchange_kernel, out_shape=(jax.ShapeDtypeStruct(extended....  73.8 us
    pallas_call x1, Pallas kernels, fold(): pl.pallas_call(fold_kernel, out_shape=(jax.ShapeDtypeStruct((2, tile, til...  59.4 us
    pallas_call x1, Pallas kernels, fetch(): pl.pallas_call(fetch_kernel, out_shape=(jax.ShapeDtypeStruct((2, side, si...  32.1 us
    pallas_call x2, Pallas kernels, slot_gradients(): pl.pallas_call(compute_kernel, out_shape=(jax.ShapeDtypeStruct(extended.s...  11.2 us
    unnamed x18, local copies, waits for them, and re-layouts  5.89 us

profile of v4, /device:TPU:198, one launch (start us, length us, event | category | flops | bytes accessed | tf_op | source)
XLA Modules:
  0.0 184.7 jit_solution(9695415814488118871)
XLA Ops:
  0.6 0.0 copy-start.4
  0.6 0.0 copy-start.5
  0.7 0.0 copy-start.6
  0.7 0.0 copy-start.7
  0.7 0.0 copy-start.3
  1.4 0.1 pad_add_fusion
  1.5 0.8 copy.11
  2.3 32.1 %fetch.1 = (f32[2,768,768]{2,1,0:T(8,128)}, f32[6,256,256]{2,1,0:T(8,128)}) custom-call(f32[2,512,512]{2,1,0:T(8,128)} %specimen.1, f32[1,6,256,256]{3,2,1,0:T(8,128)} %patterns.1), custom_call_target="tpu_custom_call" | custom-call | tf_op jit(solution)/shard_map/fetch/pallas_call | solution.py:523
  34.3 0.0 copy-done.4
  34.4 0.0 copy-done.5
  34.4 0.0 copy-done.6
  34.4 0.0 copy-done.7
  34.4 0.0 copy-done.3
  34.4 0.0 copy-start
  34.4 2.3 %copy-done = f32[2,768,768]{2,1,0:T(8,128)S(1)} copy-done((f32[2,768,768]{2,1,0:T(8,128)S(1)}, f32[2,768,768]{2,1,0:T(8,128)}, u32[]{:S(2)}) %copy-start) | copy-done | bytes 4718616
  36.7 0.0 copy-start.1
  36.7 1.4 copy-done.1
  38.1 5.5 %slot_gradients.2 = (f32[2,768,768]{2,1,0:T(8,128)S(1)}, f32[2,256,256]{2,1,0:T(8,128)S(1)}) custom-call(s32[1]{0:T(128)} %bitcast.4.count_ref, s32[6,2]{1,0:T(8,128)S(1)} %broadcast_subtract_fusion.offsets_ref, f32[2,768,768]{2,1,0:T(8,128)S(1)} %copy-done, f32[2,256,256]{2,1,0:T(8,128)S(1)} %copy-done.3, f32[6,256,256]{2,1,0:T(8,128)S(1)} %copy-done.1, ...), custom_call_target="tpu_custom_call" | custom-call | tf_op jit(solution)/shard_map/slot_gradients/pallas_call | solution.py:230
  43.6 0.0 copy-start.2
  43.6 73.8 %exchange.1 = (f32[2,768,768]{2,1,0:T(8,128)S(1)}, f32[2,256,256]{2,1,0:T(8,128)S(1)}) custom-call(f32[2,768,768]{2,1,0:T(8,128)S(1)} %get-tuple-element.12.grad, f32[2,768,768]{2,1,0:T(8,128)S(1)} %copy-done, f32[2,256,256]{2,1,0:T(8,128)S(1)} %copy-done.3, f32[2,256,256]{2,1,0:T(8,128)S(1)} %get-tuple-element.13.probe_grad), custom_call_target="tpu_custom_call" | custom-call | tf_op jit(solution)/shard_map/exchange/pallas_call | solution.py:898
  117.5 0.0 copy-done.2
  117.5 5.7 %slot_gradients.3 = (f32[2,768,768]{2,1,0:T(8,128)S(1)}, f32[2,256,256]{2,1,0:T(8,128)S(1)}) custom-call(s32[1]{0:T(128)} %bitcast.5.count_ref, s32[6,2]{1,0:T(8,128)S(1)} %broadcast_subtract_fusion.offsets_ref, f32[2,768,768]{2,1,0:T(8,128)S(1)} %get-tuple-element.14.specimen_ref.extended, f32[2,256,256]{2,1,0:T(8,128)S(1)} %get-tuple-element.15.probe_ref.probe, ...), custom_call_target="tpu_custom_call" | custom-call | tf_op jit(solution)/shard_map/slot_gradients/pallas_call | solution.py:230
  123.1 59.4 %fold.1 = (f32[2,512,512]{2,1,0:T(8,128)S(1)}, f32[2,256,256]{2,1,0:T(8,128)S(1)}) custom-call(f32[2,768,768]{2,1,0:T(8,128)S(1)} %get-tuple-element.16.grad, f32[2,768,768]{2,1,0:T(8,128)S(1)} %get-tuple-element.14.specimen_ref.extended, f32[2,256,256]{2,1,0:T(8,128)S(1)} %get-tuple-element.15.probe_ref.probe, f32[2,256,256]{2,1,0:T(8,128)S(1)} %get-tuple-element.17.probe_grad), custom_call_target="tpu_custom_call" | custom-call | tf_op jit(solution)/shard_map/fold/pallas_call | solution.py:1029
  182.6 1.3 copy.15
  183.9 0.8 copy.16
  (1 shorter events, 0.0 us)
Async XLA Ops:
  0.6 33.7 %copy-start.4 = (bf16[256,256]{1,0:T(8,128)(2,1)S(1)}, bf16[256,256]{1,0:T(8,128)(2,1)}, u32[]{:S(2)}) copy-start(bf16[256,256]{1,0:T(8,128)(2,1)} %constant.20.clone.low_t_ref) | copy-start | bytes 393220
  0.6 33.7 %copy-start.5 = (bf16[256,256]{1,0:T(8,128)(2,1)S(1)}, bf16[256,256]{1,0:T(8,128)(2,1)}, u32[]{:S(2)}) copy-start(bf16[256,256]{1,0:T(8,128)(2,1)} %constant.19.clone.high_t_ref) | copy-start | bytes 393220
  0.7 33.7 %copy-start.6 = (bf16[256,256]{1,0:T(8,128)(2,1)S(1)}, bf16[256,256]{1,0:T(8,128)(2,1)}, u32[]{:S(2)}) copy-start(bf16[256,256]{1,0:T(8,128)(2,1)} %constant.18.clone.low_ref) | copy-start | bytes 393220
  0.7 33.7 %copy-start.7 = (bf16[256,256]{1,0:T(8,128)(2,1)S(1)}, bf16[256,256]{1,0:T(8,128)(2,1)}, u32[]{:S(2)}) copy-start(bf16[256,256]{1,0:T(8,128)(2,1)} %constant.17.clone.high_ref) | copy-start | bytes 393220
  0.7 33.7 %copy-start.3 = (f32[2,256,256]{2,1,0:T(8,128)S(1)}, f32[2,256,256]{2,1,0:T(8,128)}, u32[]{:S(2)}) copy-start(f32[2,256,256]{2,1,0:T(8,128)} %probe.1) | copy-start | bytes 1572868
  34.4 2.3 %copy-start = (f32[2,768,768]{2,1,0:T(8,128)S(1)}, f32[2,768,768]{2,1,0:T(8,128)}, u32[]{:S(2)}) copy-start(f32[2,768,768]{2,1,0:T(8,128)} %get-tuple-element.10.specimen_ref.extended) | copy-start | bytes 14155780
  36.7 1.4 copy-start.1
  43.6 73.8 %copy-start.2 = (f32[6,256,256]{2,1,0:T(8,128)S(1)}, f32[6,256,256]{2,1,0:T(8,128)}, u32[]{:S(2)}) copy-start(f32[6,256,256]{2,1,0:T(8,128)} %get-tuple-element.11.measured_ref) | copy-start | bytes 4718596

commit v5 on v4

--- a/solution.py
+++ b/solution.py
@@ -763,11 +763,8 @@
     total.across_x()
     late = boundary.at_low | boundary.at_high
 
-    @pl.when(late)
-    def _():
-        total.gather_z()
-        total.gather_y()
-
+    total.gather_z()
+    pl.when(late)(total.gather_y)
     load_grad.wait()
     right_top.wait_recv()
     right_end.wait_recv()
@@ -790,11 +787,7 @@
     pl.when(has_down & odd)(down_2.start)
     pl.when(has_up & odd)(up_2.start)
 
-    @pl.when(~late)
-    def _():
-        total.gather_z()
-        total.gather_y()
-
+    pl.when(~late)(total.gather_y)
     for strip in outer:
         strip.wait_send()
     right_mid.start_direct()

time: 187 us -> 184 us (0.984)
  Pallas kernels: 176 us -> 174 us
    pallas_call x2, Pallas kernels: 11.2 us -> 20.1 us  [slot_gradients(): pl.pallas_call(compute_kernel, out_shape=(jax.ShapeDtypeStruct(extended.s...]
    pallas_call x1, Pallas kernels: 73.8 us -> 66.3 us  [exchange(): pl.pallas_call(exchange_kernel, out_shape=(jax.ShapeDtypeStruct(extended....]
    pallas_call x1, Pallas kernels: 59.4 us -> 55.3 us  [fold(): pl.pallas_call(fold_kernel, out_shape=(jax.ShapeDtypeStruct((2, tile, til...]
where the time goes in v5:
time: 184 us; the launch traced here: 182 us
  Pallas kernels  174 us (95%)
  local copies, waits for them, and re-layouts  6.65 us (4%)
    pallas_call x1, Pallas kernels, exchange(): pl.pallas_call(exchange_kernel, out_shape=(jax.ShapeDtypeStruct(extended....  66.3 us
    pallas_call x1, Pallas kernels, fold(): pl.pallas_call(fold_kernel, out_shape=(jax.ShapeDtypeStruct((2, tile, til...  55.3 us
    pallas_call x1, Pallas kernels, fetch(): pl.pallas_call(fetch_kernel, out_shape=(jax.ShapeDtypeStruct((2, side, si...  32.1 us
    pallas_call x2, Pallas kernels, slot_gradients(): pl.pallas_call(compute_kernel, out_shape=(jax.ShapeDtypeStruct(extended.s...  20.1 us
    unnamed x18, local copies, waits for them, and re-layouts  5.89 us

profile of v5, /device:TPU:198, one launch (start us, length us, event | category | flops | bytes accessed | tf_op | source)
XLA Modules:
  0.0 182.0 jit_solution(17175155305249767498)
XLA Ops:
  0.6 0.0 copy-start.4
  0.6 0.0 copy-start.5
  0.7 0.0 copy-start.6
  0.7 0.0 copy-start.7
  0.7 0.0 copy-start.3
  1.4 0.1 pad_add_fusion
  1.5 0.8 copy.11
  2.3 32.1 %fetch.1 = (f32[2,768,768]{2,1,0:T(8,128)}, f32[6,256,256]{2,1,0:T(8,128)}) custom-call(f32[2,512,512]{2,1,0:T(8,128)} %specimen.1, f32[1,6,256,256]{3,2,1,0:T(8,128)} %patterns.1), custom_call_target="tpu_custom_call" | custom-call | tf_op jit(solution)/shard_map/fetch/pallas_call | solution.py:523
  34.3 0.0 copy-done.4
  34.4 0.0 copy-done.5
  34.4 0.0 copy-done.6
  34.4 0.0 copy-done.7
  34.4 0.0 copy-done.3
  34.4 0.0 copy-start
  34.4 2.3 %copy-done = f32[2,768,768]{2,1,0:T(8,128)S(1)} copy-done((f32[2,768,768]{2,1,0:T(8,128)S(1)}, f32[2,768,768]{2,1,0:T(8,128)}, u32[]{:S(2)}) %copy-start) | copy-done | bytes 4718616
  36.7 0.0 copy-start.1
  36.7 1.4 copy-done.1
  38.1 10.0 %slot_gradients.2 = (f32[2,768,768]{2,1,0:T(8,128)S(1)}, f32[2,256,256]{2,1,0:T(8,128)S(1)}) custom-call(s32[1]{0:T(128)} %bitcast.4.count_ref, s32[6,2]{1,0:T(8,128)S(1)} %broadcast_subtract_fusion.offsets_ref, f32[2,768,768]{2,1,0:T(8,128)S(1)} %copy-done, f32[2,256,256]{2,1,0:T(8,128)S(1)} %copy-done.3, f32[6,256,256]{2,1,0:T(8,128)S(1)} %copy-done.1, ...), custom_call_target="tpu_custom_call" | custom-call | tf_op jit(solution)/shard_map/slot_gradients/pallas_call | solution.py:230
  48.1 0.0 copy-start.2
  48.1 66.3 %exchange.1 = (f32[2,768,768]{2,1,0:T(8,128)S(1)}, f32[2,256,256]{2,1,0:T(8,128)S(1)}) custom-call(f32[2,768,768]{2,1,0:T(8,128)S(1)} %get-tuple-element.12.grad, f32[2,768,768]{2,1,0:T(8,128)S(1)} %copy-done, f32[2,256,256]{2,1,0:T(8,128)S(1)} %copy-done.3, f32[2,256,256]{2,1,0:T(8,128)S(1)} %get-tuple-element.13.probe_grad), custom_call_target="tpu_custom_call" | custom-call | tf_op jit(solution)/shard_map/exchange/pallas_call | solution.py:891
  114.5 0.0 copy-done.2
  114.5 10.1 %slot_gradients.3 = (f32[2,768,768]{2,1,0:T(8,128)S(1)}, f32[2,256,256]{2,1,0:T(8,128)S(1)}) custom-call(s32[1]{0:T(128)} %bitcast.5.count_ref, s32[6,2]{1,0:T(8,128)S(1)} %broadcast_subtract_fusion.offsets_ref, f32[2,768,768]{2,1,0:T(8,128)S(1)} %get-tuple-element.14.specimen_ref.extended, f32[2,256,256]{2,1,0:T(8,128)S(1)} %get-tuple-element.15.probe_ref.probe, ...), custom_call_target="tpu_custom_call" | custom-call | tf_op jit(solution)/shard_map/slot_gradients/pallas_call | solution.py:230
  124.6 55.3 %fold.1 = (f32[2,512,512]{2,1,0:T(8,128)S(1)}, f32[2,256,256]{2,1,0:T(8,128)S(1)}) custom-call(f32[2,768,768]{2,1,0:T(8,128)S(1)} %get-tuple-element.16.grad, f32[2,768,768]{2,1,0:T(8,128)S(1)} %get-tuple-element.14.specimen_ref.extended, f32[2,256,256]{2,1,0:T(8,128)S(1)} %get-tuple-element.15.probe_ref.probe, f32[2,256,256]{2,1,0:T(8,128)S(1)} %get-tuple-element.17.probe_grad), custom_call_target="tpu_custom_call" | custom-call | tf_op jit(solution)/shard_map/fold/pallas_call | solution.py:1022
  179.9 1.3 copy.15
  181.2 0.8 copy.16
  (1 shorter events, 0.0 us)
Async XLA Ops:
  0.6 33.7 %copy-start.4 = (bf16[256,256]{1,0:T(8,128)(2,1)S(1)}, bf16[256,256]{1,0:T(8,128)(2,1)}, u32[]{:S(2)}) copy-start(bf16[256,256]{1,0:T(8,128)(2,1)} %constant.20.clone.low_t_ref) | copy-start | bytes 393220
  0.6 33.7 %copy-start.5 = (bf16[256,256]{1,0:T(8,128)(2,1)S(1)}, bf16[256,256]{1,0:T(8,128)(2,1)}, u32[]{:S(2)}) copy-start(bf16[256,256]{1,0:T(8,128)(2,1)} %constant.19.clone.high_t_ref) | copy-start | bytes 393220
  0.7 33.7 %copy-start.6 = (bf16[256,256]{1,0:T(8,128)(2,1)S(1)}, bf16[256,256]{1,0:T(8,128)(2,1)}, u32[]{:S(2)}) copy-start(bf16[256,256]{1,0:T(8,128)(2,1)} %constant.18.clone.low_ref) | copy-start | bytes 393220
  0.7 33.7 %copy-start.7 = (bf16[256,256]{1,0:T(8,128)(2,1)S(1)}, bf16[256,256]{1,0:T(8,128)(2,1)}, u32[]{:S(2)}) copy-start(bf16[256,256]{1,0:T(8,128)(2,1)} %constant.17.clone.high_ref) | copy-start | bytes 393220
  0.7 33.7 %copy-start.3 = (f32[2,256,256]{2,1,0:T(8,128)S(1)}, f32[2,256,256]{2,1,0:T(8,128)}, u32[]{:S(2)}) copy-start(f32[2,256,256]{2,1,0:T(8,128)} %probe.1) | copy-start | bytes 1572868
  34.4 2.3 %copy-start = (f32[2,768,768]{2,1,0:T(8,128)S(1)}, f32[2,768,768]{2,1,0:T(8,128)}, u32[]{:S(2)}) copy-start(f32[2,768,768]{2,1,0:T(8,128)} %get-tuple-element.10.specimen_ref.extended) | copy-start | bytes 14155780
  36.7 1.4 copy-start.1
  48.1 66.4 %copy-start.2 = (f32[6,256,256]{2,1,0:T(8,128)S(1)}, f32[6,256,256]{2,1,0:T(8,128)}, u32[]{:S(2)}) copy-start(f32[6,256,256]{2,1,0:T(8,128)} %get-tuple-element.11.measured_ref) | copy-start | bytes 4718596

commit v6 on v5

--- a/solution.py
+++ b/solution.py
@@ -954,12 +954,9 @@
     right_top.pass_on()
     load_grad.wait()
 
-    @pl.when(boundary.at_high)
-    def _():
-        total.across_x()
-        total.gather_z()
-        total.gather_y()
-
+    total.across_x()
+    total.gather_z()
+    pl.when(boundary.at_high)(total.gather_y)
     right_end.wait_recv()
 
     @pl.when(has_left)
@@ -970,17 +967,8 @@
     def _():
         corner[...] = gv[:, end, start]
 
-    @pl.when(~boundary.at_high)
-    def _():
-        total.across_x()
-
     pl.when(has_down)(down_0.start)
-
-    @pl.when(~boundary.at_high)
-    def _():
-        total.gather_z()
-        total.gather_y()
-
+    pl.when(~boundary.at_high)(total.gather_y)
     right_end.wait_send()
     right_mid.start_direct()
     right_mid.pass_on()

time: 184 us -> 183 us (level)
  Pallas kernels: 174 us -> 172 us
    pallas_call x2, Pallas kernels: 20.1 us -> 11.2 us  [slot_gradients(): pl.pallas_call(compute_kernel, out_shape=(jax.ShapeDtypeStruct(extended.s...]
    pallas_call x1, Pallas kernels: 66.3 us -> 72.9 us  [exchange(): pl.pallas_call(exchange_kernel, out_shape=(jax.ShapeDtypeStruct(extended....]
where the time goes in v6:
time: 183 us; the launch traced here: 181 us
  Pallas kernels  172 us (94%)
  local copies, waits for them, and re-layouts  6.65 us (4%)
    pallas_call x1, Pallas kernels, exchange(): pl.pallas_call(exchange_kernel, out_shape=(jax.ShapeDtypeStruct(extended....  72.9 us
    pallas_call x1, Pallas kernels, fold(): pl.pallas_call(fold_kernel, out_shape=(jax.ShapeDtypeStruct((2, tile, til...  56.2 us
    pallas_call x1, Pallas kernels, fetch(): pl.pallas_call(fetch_kernel, out_shape=(jax.ShapeDtypeStruct((2, side, si...  32.1 us
    pallas_call x2, Pallas kernels, slot_gradients(): pl.pallas_call(compute_kernel, out_shape=(jax.ShapeDtypeStruct(extended.s...  11.2 us
    unnamed x18, local copies, waits for them, and re-layouts  5.89 us

profile of v6, /device:TPU:198, one launch (start us, length us, event | category | flops | bytes accessed | tf_op | source)
XLA Modules:
  0.0 180.6 jit_solution(15495080160976609699)
XLA Ops:
  0.6 0.0 copy-start.4
  0.6 0.0 copy-start.5
  0.7 0.0 copy-start.6
  0.7 0.0 copy-start.7
  0.7 0.0 copy-start.3
  1.4 0.1 pad_add_fusion
  1.5 0.8 copy.11
  2.3 32.1 %fetch.1 = (f32[2,768,768]{2,1,0:T(8,128)}, f32[6,256,256]{2,1,0:T(8,128)}) custom-call(f32[2,512,512]{2,1,0:T(8,128)} %specimen.1, f32[1,6,256,256]{3,2,1,0:T(8,128)} %patterns.1), custom_call_target="tpu_custom_call" | custom-call | tf_op jit(solution)/shard_map/fetch/pallas_call | solution.py:523
  34.3 0.0 copy-done.4
  34.4 0.0 copy-done.5
  34.4 0.0 copy-done.6
  34.4 0.0 copy-done.7
  34.4 0.0 copy-done.3
  34.4 0.0 copy-start
  34.4 2.3 %copy-done = f32[2,768,768]{2,1,0:T(8,128)S(1)} copy-done((f32[2,768,768]{2,1,0:T(8,128)S(1)}, f32[2,768,768]{2,1,0:T(8,128)}, u32[]{:S(2)}) %copy-start) | copy-done | bytes 4718616
  36.7 0.0 copy-start.1
  36.7 1.4 copy-done.1
  38.1 5.5 %slot_gradients.2 = (f32[2,768,768]{2,1,0:T(8,128)S(1)}, f32[2,256,256]{2,1,0:T(8,128)S(1)}) custom-call(s32[1]{0:T(128)} %bitcast.4.count_ref, s32[6,2]{1,0:T(8,128)S(1)} %broadcast_subtract_fusion.offsets_ref, f32[2,768,768]{2,1,0:T(8,128)S(1)} %copy-done, f32[2,256,256]{2,1,0:T(8,128)S(1)} %copy-done.3, f32[6,256,256]{2,1,0:T(8,128)S(1)} %copy-done.1, ...), custom_call_target="tpu_custom_call" | custom-call | tf_op jit(solution)/shard_map/slot_gradients/pallas_call | solution.py:230
  43.6 0.0 copy-start.2
  43.7 72.9 %exchange.1 = (f32[2,768,768]{2,1,0:T(8,128)S(1)}, f32[2,256,256]{2,1,0:T(8,128)S(1)}) custom-call(f32[2,768,768]{2,1,0:T(8,128)S(1)} %get-tuple-element.12.grad, f32[2,768,768]{2,1,0:T(8,128)S(1)} %copy-done, f32[2,256,256]{2,1,0:T(8,128)S(1)} %copy-done.3, f32[2,256,256]{2,1,0:T(8,128)S(1)} %get-tuple-element.13.probe_grad), custom_call_target="tpu_custom_call" | custom-call | tf_op jit(solution)/shard_map/exchange/pallas_call | solution.py:891
  116.6 0.0 copy-done.2
  116.6 5.7 %slot_gradients.3 = (f32[2,768,768]{2,1,0:T(8,128)S(1)}, f32[2,256,256]{2,1,0:T(8,128)S(1)}) custom-call(s32[1]{0:T(128)} %bitcast.5.count_ref, s32[6,2]{1,0:T(8,128)S(1)} %broadcast_subtract_fusion.offsets_ref, f32[2,768,768]{2,1,0:T(8,128)S(1)} %get-tuple-element.14.specimen_ref.extended, f32[2,256,256]{2,1,0:T(8,128)S(1)} %get-tuple-element.15.probe_ref.probe, ...), custom_call_target="tpu_custom_call" | custom-call | tf_op jit(solution)/shard_map/slot_gradients/pallas_call | solution.py:230
  122.3 56.2 %fold.1 = (f32[2,512,512]{2,1,0:T(8,128)S(1)}, f32[2,256,256]{2,1,0:T(8,128)S(1)}) custom-call(f32[2,768,768]{2,1,0:T(8,128)S(1)} %get-tuple-element.16.grad, f32[2,768,768]{2,1,0:T(8,128)S(1)} %get-tuple-element.14.specimen_ref.extended, f32[2,256,256]{2,1,0:T(8,128)S(1)} %get-tuple-element.15.probe_ref.probe, f32[2,256,256]{2,1,0:T(8,128)S(1)} %get-tuple-element.17.probe_grad), custom_call_target="tpu_custom_call" | custom-call | tf_op jit(solution)/shard_map/fold/pallas_call | solution.py:1010
  178.5 1.3 copy.15
  179.8 0.8 copy.16
  (1 shorter events, 0.0 us)
Async XLA Ops:
  0.6 33.7 %copy-start.4 = (bf16[256,256]{1,0:T(8,128)(2,1)S(1)}, bf16[256,256]{1,0:T(8,128)(2,1)}, u32[]{:S(2)}) copy-start(bf16[256,256]{1,0:T(8,128)(2,1)} %constant.20.clone.low_t_ref) | copy-start | bytes 393220
  0.6 33.7 %copy-start.5 = (bf16[256,256]{1,0:T(8,128)(2,1)S(1)}, bf16[256,256]{1,0:T(8,128)(2,1)}, u32[]{:S(2)}) copy-start(bf16[256,256]{1,0:T(8,128)(2,1)} %constant.19.clone.high_t_ref) | copy-start | bytes 393220
  0.7 33.7 %copy-start.6 = (bf16[256,256]{1,0:T(8,128)(2,1)S(1)}, bf16[256,256]{1,0:T(8,128)(2,1)}, u32[]{:S(2)}) copy-start(bf16[256,256]{1,0:T(8,128)(2,1)} %constant.18.clone.low_ref) | copy-start | bytes 393220
  0.7 33.7 %copy-start.7 = (bf16[256,256]{1,0:T(8,128)(2,1)S(1)}, bf16[256,256]{1,0:T(8,128)(2,1)}, u32[]{:S(2)}) copy-start(bf16[256,256]{1,0:T(8,128)(2,1)} %constant.17.clone.high_ref) | copy-start | bytes 393220
  0.7 33.7 %copy-start.3 = (f32[2,256,256]{2,1,0:T(8,128)S(1)}, f32[2,256,256]{2,1,0:T(8,128)}, u32[]{:S(2)}) copy-start(f32[2,256,256]{2,1,0:T(8,128)} %probe.1) | copy-start | bytes 1572868
  34.4 2.3 %copy-start = (f32[2,768,768]{2,1,0:T(8,128)S(1)}, f32[2,768,768]{2,1,0:T(8,128)}, u32[]{:S(2)}) copy-start(f32[2,768,768]{2,1,0:T(8,128)} %get-tuple-element.10.specimen_ref.extended) | copy-start | bytes 14155780
  36.7 1.4 copy-start.1
  43.6 73.0 %copy-start.2 = (f32[6,256,256]{2,1,0:T(8,128)S(1)}, f32[6,256,256]{2,1,0:T(8,128)}, u32[]{:S(2)}) copy-start(f32[6,256,256]{2,1,0:T(8,128)} %get-tuple-element.11.measured_ref) | copy-start | bytes 4718596
